TPU v7x, 32 devices: a whole 2x2x4 slice. The times are simulated.
32 devices in a mesh: gr: 8 (over y, x, core), gc: 4 (over z).
Axes of the slice: x: 2, y: 2, z: 4, core: 2. Of those that a mesh axis runs over, the one named last changes fastest.
Arguments:
- queries: bfloat16 [64, 64, 8, 128], P('gr', 'gc'), may hold values from -6 to 6
- key_vectors: bfloat16 [64, 64, 8, 128], P('gr', 'gc'), may hold values from -6 to 6
- values: bfloat16 [64, 64, 8, 128], P('gr', 'gc'), may hold values from -6 to 6
- strength: bfloat16 [64, 64, 8], P('gr', 'gc'), may hold values from 0.099609375 to 0.8984375
- decay_rate: bfloat16 [64, 64, 8], P('gr', 'gc'), may hold values from 0 to 1, as said below
- out_grad: bfloat16 [64, 64, 8, 128], P('gr', 'gc'), may hold values from -6 to 6
Outputs:
- query_grad: bfloat16 [64, 64, 8, 128], P('gr', 'gc')
- key_grad: bfloat16 [64, 64, 8, 128], P('gr', 'gc')
- value_grad: bfloat16 [64, 64, 8, 128], P('gr', 'gc')
- strength_grad: bfloat16 [64, 64, 8], P('gr', 'gc')
- decay_grad: bfloat16 [64, 64, 8], P('gr', 'gc')
Inputs may be any that keep to these rules, and one draw needn't show every extreme that they name: decay_rate is positive: the state keeps exp(-decay_rate) of itself at each token.
All inputs are finite; a program needn't handle non-finite values.
Results may differ from a plain program's by a relative error of at most 0.0051.
Values may be sent and summed in bfloat16 or wider, within the bound.
A program may use at most 128 MiB of HBM per device.

v0:
```python
import jax
import jax.numpy as jnp
from jax import lax
from jax.sharding import PartitionSpec as P

block_len = 64
doubling_rounds = 5
highest = lax.Precision.HIGHEST


def as_sent(value):
    return jax.tree.map(lambda a: a.astype(jnp.bfloat16) if a.dtype == jnp.float32 else a, value)


def normalize(tensor):
    return tensor / jnp.sqrt(jnp.sum(tensor * tensor, axis=-1, keepdims=True) + 1e-06)


def stretch_forward(queries, keys_in, values, gains, decays):
    length = queries.shape[0]
    lines_count = queries.shape[1]
    head_size = queries.shape[2]
    blocks_count = length // block_len

    def split_blocks(tensor):
        shaped = tensor.reshape((blocks_count, block_len) + tensor.shape[1:])
        return jnp.swapaxes(shaped, 1, 2)

    log_decay = jnp.cumsum(-split_blocks(decays), axis=-1)
    offsets = jnp.arange(block_len)
    strict = offsets[:, None] > offsets[None, :]
    inclusive = offsets[:, None] >= offsets[None, :]
    identity = jnp.eye(block_len, dtype=jnp.float32)

    def advance(state, slices):
        query_block, key_block, value_block, gain_block, decay_block = slices
        gaps = decay_block[:, :, None] - decay_block[:, None, :]
        below = jnp.where(strict, jnp.exp(jnp.where(strict, gaps, 0.0)), 0.0)
        within = jnp.where(inclusive, jnp.exp(jnp.where(inclusive, gaps, 0.0)), 0.0)
        key_key = jnp.einsum("btd,bjd->btj", key_block, key_block, precision=highest)
        lower_part = -(gain_block[:, :, None] * below * key_key)
        inverse = identity + lower_part
        power = lower_part
        for round_index in range(doubling_rounds):
            power = jnp.einsum("btj,bjs->bts", power, power, precision=highest)
            inverse = inverse + jnp.einsum("btj,bjs->bts", power, inverse, precision=highest)
        leading = jnp.exp(decay_block)[:, :, None]
        carried = jnp.einsum("btd,bde->bte", key_block, state, precision=highest)
        right_side = gain_block[:, :, None] * (value_block - leading * carried)
        writes = jnp.einsum("btj,bje->bte", inverse, right_side, precision=highest)
        query_key = jnp.einsum("btd,bjd->btj", query_block, key_block, precision=highest)
        outputs = leading * jnp.einsum("btd,bde->bte", query_block, state, precision=highest)
        outputs = outputs + jnp.einsum(
            "btj,bje->bte", within * query_key, writes, precision=highest
        )
        trailing = jnp.exp(decay_block[:, -1:] - decay_block)[:, :, None]
        updated = jnp.exp(decay_block[:, -1])[:, None, None] * state
        updated = updated + jnp.einsum(
            "bjd,bje->bde", key_block * trailing, writes, precision=highest
        )
        return (updated, outputs)

    state = jnp.zeros((lines_count, head_size, values.shape[-1]), jnp.float32)
    slices = (
        split_blocks(queries),
        split_blocks(keys_in),
        split_blocks(values),
        split_blocks(gains),
        log_decay,
    )
    outputs = lax.scan(jax.checkpoint(advance), state, slices)[1]
    return jnp.swapaxes(outputs, 1, 2).reshape((length, lines_count, values.shape[-1]))


def directed(queries, keys_in, values, gains, decays, seq_dim):

    def as_lines(tensor):
        moved = jnp.moveaxis(tensor, seq_dim, 0)
        return moved.reshape((moved.shape[0], -1) + moved.shape[3:])

    outputs = stretch_forward(
        as_lines(normalize(queries)),
        as_lines(normalize(keys_in)),
        as_lines(values),
        as_lines(gains),
        as_lines(decays),
    )
    moved_shape = jnp.moveaxis(values, seq_dim, 0).shape
    return jnp.moveaxis(outputs.reshape(moved_shape), 0, seq_dim)


def pair_grads(pieces, seq_dim):
    queries, keys_in, values, out_grad, gains, decays = pieces
    other_dim = 1 - seq_dim

    def two_ways(query_f, key_f, value_f, gain_f, decay_f):

        def both(tensor):
            return jnp.concatenate([tensor, jnp.flip(tensor, seq_dim)], axis=other_dim)

        joined = directed(
            both(query_f), both(key_f), both(value_f), both(gain_f), both(decay_f), seq_dim
        )
        half = query_f.shape[other_dim]
        forward = lax.slice_in_dim(joined, 0, half, axis=other_dim)
        backward = lax.slice_in_dim(joined, half, 2 * half, axis=other_dim)
        return forward + jnp.flip(backward, seq_dim)

    primals = tuple(
        (tensor.astype(jnp.float32) for tensor in (queries, keys_in, values, gains, decays))
    )
    pullback = jax.vjp(two_ways, *primals)[1]
    gradients = pullback(out_grad.astype(jnp.float32))
    return tuple((member.astype(jnp.bfloat16) for member in gradients))


def on_device(queries, key_vectors, values, strength, decay_rate, out_grad):
    inputs = (queries, key_vectors, values, out_grad, strength, decay_rate)
    arrived = (
        lax.all_to_all(inputs[0], "gc", split_axis=0, concat_axis=1, tiled=True),
        lax.all_to_all(inputs[1], "gc", split_axis=0, concat_axis=1, tiled=True),
        lax.all_to_all(inputs[2], "gc", split_axis=0, concat_axis=1, tiled=True),
        lax.all_to_all(inputs[3], "gc", split_axis=0, concat_axis=1, tiled=True),
        lax.all_to_all(inputs[4], "gc", split_axis=0, concat_axis=1, tiled=True),
        lax.all_to_all(inputs[5], "gc", split_axis=0, concat_axis=1, tiled=True),
    )
    row_grads = lax.all_to_all(
        as_sent(pair_grads(arrived, 1)), "gc", split_axis=1, concat_axis=0, tiled=True
    )
    arrived = (
        lax.all_to_all(inputs[0], "gr", split_axis=1, concat_axis=0, tiled=True),
        lax.all_to_all(inputs[1], "gr", split_axis=1, concat_axis=0, tiled=True),
        lax.all_to_all(inputs[2], "gr", split_axis=1, concat_axis=0, tiled=True),
        lax.all_to_all(inputs[3], "gr", split_axis=1, concat_axis=0, tiled=True),
        lax.all_to_all(inputs[4], "gr", split_axis=1, concat_axis=0, tiled=True),
        lax.all_to_all(inputs[5], "gr", split_axis=1, concat_axis=0, tiled=True),
    )
    column_grads = lax.all_to_all(
        as_sent(pair_grads(arrived, 0)), "gr", split_axis=0, concat_axis=1, tiled=True
    )
    merged = [
        (first.astype(jnp.float32) + second.astype(jnp.float32)).astype(jnp.bfloat16)
        for first, second in zip(row_grads, column_grads)
    ]
    return (merged[0], merged[1], merged[2], merged[3], merged[4])


def solution(mesh):
    return jax.shard_map(
        on_device,
        mesh=mesh,
        in_specs=(
            P("gr", "gc", None, None),
            P("gr", "gc", None, None),
            P("gr", "gc", None, None),
            P("gr", "gc", None),
            P("gr", "gc", None),
            P("gr", "gc", None, None),
        ),
        out_specs=(
            P("gr", "gc", None, None),
            P("gr", "gc", None, None),
            P("gr", "gc", None, None),
            P("gr", "gc", None),
            P("gr", "gc", None),
        ),
        check_vma=False,
    )
```

profile of v0, /device:TPU:0, one launch (start us, length us, event | category | flops | bytes accessed | tf_op | source)
XLA Modules:
  0.0 492.7 jit_solution(5540659356388119793)
XLA Ops:
  2.1 5.2 %all-to-all-start.10 = ((bf16[8,16,8]{2,0,1:T(8,128)(2,1)}), bf16[8,16,8]{2,0,1:T(8,128)(2,1)S(1)}, u32[]{:S(2)}, u32[]{:S(2)}) async-start(bf16[8,16,8]{2,0,1:T(8,128)(2,1)} %copy.1010), calls=%async_computation.10 | async-start | bytes 65536 | tf_op jit(solution)/shard_map/all_to_all | solution.py:135
  17.0 4.2 all-to-all-start.11
  21.2 4.8 all-to-all-done.11
  26.0 4.9 all-to-all-start.3
  31.2 5.2 %all-to-all-done.3 = bf16[4,2,128]{2,1,0:T(2,128)(2,1)S(1)} async-done(((bf16[4,2,128]{2,1,0:T(2,128)(2,1)}), bf16[4,2,128]{2,1,0:T(2,128)(2,1)S(1)}, u32[]{:S(2)}, u32[]{:S(2)}) %all-to-all-start.3) | async-done | bytes 2080 | tf_op jit(solution)/shard_map/all_to_all | solution.py:124
  39.9 5.2 %all-to-all-done.4 = bf16[4,2,128]{2,1,0:T(2,128)(2,1)S(1)} async-done(((bf16[4,2,128]{2,1,0:T(2,128)(2,1)}), bf16[4,2,128]{2,1,0:T(2,128)(2,1)S(1)}, u32[]{:S(2)}, u32[]{:S(2)}) %all-to-all-start.4) | async-done | bytes 2080 | tf_op jit(solution)/shard_map/all_to_all | solution.py:125
  49.4 5.9 %all-to-all-done.7 = bf16[8,16,8,128]{3,2,0,1:T(8,128)(2,1)S(1)} async-done(((bf16[8,16,8,128]{3,2,0,1:T(8,128)(2,1)}), bf16[8,16,8,128]{3,2,0,1:T(8,128)(2,1)S(1)}, u32[]{:S(2)}, u32[]{:S(2)}) %all-to-all-start.7) | async-done | bytes 262176 | tf_op jit(solution)/shard_map/all_to_all | solution.py:131
  61.0 4.7 all-to-all-done.8
  71.9 4.0 all-to-all-done.9
  108.5 5.1 %fusion.58 = f32[32,64,128]{2,1,0:T(8,128)} fusion(f32[32,128,128]{2,1,0:T(8,128)S(1)} %squeeze.95, f32[32,64,128]{2,1,0:T(8,128)S(1)} %bitcast.497, f32[32,64]{1,0:T(8,128)S(1)} %copy.1017), kind=kOutput, calls=%fused_computation.139 | convolution fusion | flops 402915328 | bytes 4202496 | tf_op jit(solution)/shard_map/transpose(jvp())/while/body/eval_jaxpr/checkpoint/btd,bde->bte/dot_general | solution.py:52
  122.4 5.1 %multiply_reduce_fusion.3 = (f32[32,64]{1,0:T(8,128)S(1)}, f32[32,64,128]{2,1,0:T(8,128)}) fusion(f32[32,64,128]{2,1,0:T(8,128)S(1)} %divide_bitcast_fusion, f32[32,64,128]{2,1,0:T(8,128)S(1)} %fusion.66, f32[32,128,128]{2,1,0:T(8,128)S(1)} %squeeze.95), kind=kOutput, calls=%fused_computation.127 | convolution fusion | flops 403175424 | bytes 5251072 | tf_op jit(solution)/shard_map/transpose(jvp())/while/body/eval_jaxpr/checkpoint/bjd,bje->bde/dot_general | solution.py:58
  174.1 3.9 fusion.33
  178.1 3.9 fusion.49
  183.1 4.7 multiply_reduce_fusion.2
  189.5 4.1 convolution_add_fusion.30
  202.4 4.0 all-to-all-start.19
  221.1 5.9 %all-to-all-done = bf16[8,16,8,128]{3,2,1,0:T(8,128)(2,1)S(1)} async-done(((bf16[8,16,8,128]{3,2,1,0:T(8,128)(2,1)}), bf16[8,16,8,128]{3,2,1,0:T(8,128)(2,1)S(1)}, u32[]{:S(2)}, u32[]{:S(2)}) %all-to-all-start) | async-done | bytes 262176 | tf_op jit(solution)/shard_map/all_to_all | solution.py:120
  227.0 4.0 all-to-all-start.1
  239.2 4.0 all-to-all-start.2
  250.1 5.0 %all-to-all-start.5 = ((bf16[8,16,8,128]{3,2,1,0:T(8,128)(2,1)}), bf16[8,16,8,128]{3,2,1,0:T(8,128)(2,1)}, u32[]{:S(2)}, u32[]{:S(2)}) async-start(bf16[8,16,8,128]{3,2,1,0:T(8,128)(2,1)} %param.11), calls=%async_computation.5 | async-start | bytes 524288 | tf_op jit(solution)/shard_map/all_to_all | solution.py:123
  293.9 5.1 %fusion.60 = f32[32,64,128]{2,1,0:T(8,128)} fusion(f32[32,128,128]{2,1,0:T(8,128)S(1)} %squeeze.95, f32[32,64,128]{2,1,0:T(8,128)S(1)} %bitcast.501, f32[32,64]{1,0:T(8,128)S(1)} %copy.979), kind=kOutput, calls=%fused_computation.147 | convolution fusion | flops 402915328 | bytes 4202496 | tf_op jit(solution)/shard_map/transpose(jvp())/while/body/eval_jaxpr/checkpoint/btd,bde->bte/dot_general | solution.py:52
  308.4 5.2 %multiply_reduce_fusion.5 = (f32[32,64]{1,0:T(8,128)S(1)}, f32[32,64,128]{2,1,0:T(8,128)}) fusion(f32[32,64,128]{2,1,0:T(8,128)S(1)} %bitcast.492, f32[32,64,128]{2,1,0:T(8,128)S(1)} %fusion.72, f32[32,128,128]{2,1,0:T(8,128)S(1)} %squeeze.95), kind=kOutput, calls=%fused_computation.129 | convolution fusion | flops 403175424 | bytes 5251072 | tf_op jit(solution)/shard_map/transpose(jvp())/while/body/eval_jaxpr/checkpoint/bjd,bje->bde/dot_general | solution.py:58
  363.0 4.2 fusion.15
  386.5 4.1 convolution_add_fusion.43
  408.2 5.1 %all-to-all-start.18 = ((bf16[4,2,128]{2,1,0:T(2,128)(2,1)}), bf16[4,2,128]{2,1,0:T(2,128)(2,1)S(1)}, u32[]{:S(2)}, u32[]{:S(2)}) async-start(bf16[4,2,128]{2,1,0:T(2,128)(2,1)} %reshape.580), calls=%async_computation.18 | async-start | bytes 4096 | tf_op jit(solution)/shard_map/all_to_all | solution.py:127
  414.1 4.7 all-to-all-done.18
  431.6 6.0 %all-to-all-done.13 = bf16[64,2,8,128]{3,2,1,0:T(8,128)(2,1)S(1)} async-done(((bf16[64,2,8,128]{3,2,1,0:T(8,128)(2,1)}), bf16[64,2,8,128]{3,2,1,0:T(8,128)(2,1)S(1)}, u32[]{:S(2)}, u32[]{:S(2)}) %all-to-all-start.13) | async-done | bytes 262176 | tf_op jit(solution)/shard_map/all_to_all | solution.py:138
  443.1 4.9 all-to-all-done.17
  453.6 4.6 all-to-all-done.15
  462.4 7.8 %all-to-all-done.6 = bf16[2,64,8,128]{3,2,0,1:T(8,128)(2,1)S(1)} async-done(((bf16[2,64,8,128]{3,2,0,1:T(8,128)(2,1)}), bf16[2,64,8,128]{3,2,0,1:T(8,128)(2,1)S(1)}, u32[]{:S(2)}, u32[]{:S(2)}) %all-to-all-start.6) | async-done | bytes 262176 | tf_op jit(solution)/shard_map/all_to_all | solution.py:127
  474.7 5.8 %all-to-all-done.16 = bf16[2,64,8,128]{3,2,0,1:T(8,128)(2,1)S(1)} async-done(((bf16[2,64,8,128]{3,2,0,1:T(8,128)(2,1)}), bf16[2,64,8,128]{3,2,0,1:T(8,128)(2,1)S(1)}, u32[]{:S(2)}, u32[]{:S(2)}) %all-to-all-start.16) | async-done | bytes 262176 | tf_op jit(solution)/shard_map/all_to_all | solution.py:127
  484.1 6.6 %all-to-all-done.14 = bf16[2,64,8,128]{3,2,0,1:T(8,128)(2,1)S(1)} async-done(((bf16[2,64,8,128]{3,2,0,1:T(8,128)(2,1)}), bf16[2,64,8,128]{3,2,0,1:T(8,128)(2,1)S(1)}, u32[]{:S(2)}, u32[]{:S(2)}) %all-to-all-start.14) | async-done | bytes 262176 | tf_op jit(solution)/shard_map/all_to_all | solution.py:127
  (622 shorter events, 330.8 us)
Async XLA Ops:
  0.6 15.0 %copy-start.150 = (bf16[8,16,8]{1,2,0:T(8,128)(2,1)S(1)}, bf16[8,16,8]{1,2,0:T(8,128)(2,1)}, u32[]{:S(2)}) copy-start(bf16[8,16,8]{1,2,0:T(8,128)(2,1)} %param.9) | copy-start | bytes 6148
  0.6 15.7 %copy-start.151 = (bf16[8,16,8]{1,2,0:T(8,128)(2,1)S(1)}, bf16[8,16,8]{1,2,0:T(8,128)(2,1)}, u32[]{:S(2)}) copy-start(bf16[8,16,8]{1,2,0:T(8,128)(2,1)} %param.10) | copy-start | bytes 6148
  2.1 14.9 %all-to-all-start.10 = ((bf16[8,16,8]{2,0,1:T(8,128)(2,1)}), bf16[8,16,8]{2,0,1:T(8,128)(2,1)S(1)}, u32[]{:S(2)}, u32[]{:S(2)}) async-start(bf16[8,16,8]{2,0,1:T(8,128)(2,1)} %copy.1010), calls=%async_computation.10 | async-start | bytes 65536 | tf_op jit(solution)/shard_map/all_to_all | solution.py:135
  17.0 9.0 %all-to-all-start.11 = ((bf16[8,16,8]{2,0,1:T(8,128)(2,1)}), bf16[8,16,8]{2,0,1:T(8,128)(2,1)S(1)}, u32[]{:S(2)}, u32[]{:S(2)}) async-start(bf16[8,16,8]{2,0,1:T(8,128)(2,1)} %copy.1012), calls=%async_computation.11 | async-start | bytes 65536 | tf_op jit(solution)/shard_map/all_to_all | solution.py:136
  26.0 10.3 %all-to-all-start.3 = ((bf16[4,2,128]{2,1,0:T(2,128)(2,1)}), bf16[4,2,128]{2,1,0:T(2,128)(2,1)S(1)}, u32[]{:S(2)}, u32[]{:S(2)}) async-start(bf16[4,2,128]{2,1,0:T(2,128)(2,1)} %reshape.576), calls=%async_computation.3 | async-start | bytes 4096 | tf_op jit(solution)/shard_map/all_to_all | solution.py:124
  36.4 8.7 %all-to-all-start.4 = ((bf16[4,2,128]{2,1,0:T(2,128)(2,1)}), bf16[4,2,128]{2,1,0:T(2,128)(2,1)S(1)}, u32[]{:S(2)}, u32[]{:S(2)}) async-start(bf16[4,2,128]{2,1,0:T(2,128)(2,1)} %reshape.578), calls=%async_computation.4 | async-start | bytes 4096 | tf_op jit(solution)/shard_map/all_to_all | solution.py:125
  45.0 10.3 %all-to-all-start.7 = ((bf16[8,16,8,128]{3,2,0,1:T(8,128)(2,1)}), bf16[8,16,8,128]{3,2,0,1:T(8,128)(2,1)S(1)}, u32[]{:S(2)}, u32[]{:S(2)}) async-start(bf16[8,16,8,128]{3,2,0,1:T(8,128)(2,1)} %copy.1000), calls=%async_computation.7 | async-start | bytes 524288 | tf_op jit(solution)/shard_map/all_to_all | solution.py:131
  55.3 10.3 %all-to-all-start.8 = ((bf16[8,16,8,128]{3,2,0,1:T(8,128)(2,1)}), bf16[8,16,8,128]{3,2,0,1:T(8,128)(2,1)S(1)}, u32[]{:S(2)}, u32[]{:S(2)}) async-start(bf16[8,16,8,128]{3,2,0,1:T(8,128)(2,1)} %copy.1004), calls=%async_computation.8 | async-start | bytes 524288 | tf_op jit(solution)/shard_map/all_to_all | solution.py:132
  65.6 10.3 %all-to-all-start.9 = ((bf16[8,16,8,128]{3,2,0,1:T(8,128)(2,1)}), bf16[8,16,8,128]{3,2,0,1:T(8,128)(2,1)S(1)}, u32[]{:S(2)}, u32[]{:S(2)}) async-start(bf16[8,16,8,128]{3,2,0,1:T(8,128)(2,1)} %copy.1008), calls=%async_computation.9 | async-start | bytes 524288 | tf_op jit(solution)/shard_map/all_to_all | solution.py:133
  75.9 10.3 %all-to-all-start.12 = ((bf16[8,16,8,128]{3,2,0,1:T(8,128)(2,1)}), bf16[8,16,8,128]{3,2,0,1:T(8,128)(2,1)S(1)}, u32[]{:S(2)}, u32[]{:S(2)}) async-start(bf16[8,16,8,128]{3,2,0,1:T(8,128)(2,1)} %copy.1014), calls=%async_computation.12 | async-start | bytes 524288 | tf_op jit(solution)/shard_map/all_to_all | solution.py:134
  88.4 25.3 %copy-start.123 = (f32[32,64]{1,0:T(8,128)}, f32[32,64]{1,0:T(8,128)S(1)}, u32[]{:S(2)}) copy-start(f32[32,64]{1,0:T(8,128)S(1)} %copy.1017) | copy-start | bytes 24580
  202.4 11.5 %all-to-all-start.19 = ((bf16[64,2,8]{2,1,0:T(2,128)(2,1)}), bf16[64,2,8]{2,1,0:T(2,128)(2,1)}, u32[]{:S(2)}, u32[]{:S(2)}) async-start(bf16[64,2,8]{2,1,0:T(2,128)(2,1)} %copy.1098), calls=%async_computation.19 | async-start | bytes 65536 | tf_op jit(solution)/shard_map/all_to_all | solution.py:138
  213.9 13.1 %all-to-all-start = ((bf16[8,16,8,128]{3,2,1,0:T(8,128)(2,1)}), bf16[8,16,8,128]{3,2,1,0:T(8,128)(2,1)S(1)}, u32[]{:S(2)}, u32[]{:S(2)}) async-start(bf16[8,16,8,128]{3,2,1,0:T(8,128)(2,1)} %param.6), calls=%async_computation | async-start | bytes 524288 | tf_op jit(solution)/shard_map/all_to_all | solution.py:120
  219.2 11.9 %copy-start.110 = (f32[64,2,8,128]{3,2,1,0:T(8,128)S(1)}, f32[64,2,8,128]{3,2,1,0:T(8,128)}, u32[]{:S(2)}) copy-start(f32[64,2,8,128]{3,2,1,0:T(8,128)} %copy.1194) | copy-start | bytes 1572868
  227.0 12.3 %all-to-all-start.1 = ((bf16[8,16,8,128]{3,2,1,0:T(8,128)(2,1)}), bf16[8,16,8,128]{3,2,1,0:T(8,128)(2,1)}, u32[]{:S(2)}, u32[]{:S(2)}) async-start(bf16[8,16,8,128]{3,2,1,0:T(8,128)(2,1)} %param.7), calls=%async_computation.1 | async-start | bytes 524288 | tf_op jit(solution)/shard_map/all_to_all | solution.py:121
  234.9 12.6 %copy-start.26 = (f32[4,2,16,8,128]{4,3,1,2,0:T(8,128)}, f32[4,2,16,8,128]{4,3,1,2,0:T(8,128)S(1)}, u32[]{:S(2)}) copy-start(f32[4,2,16,8,128]{4,3,1,2,0:T(8,128)S(1)} %copy.966) | copy-start | bytes 1572868
  239.2 10.9 %all-to-all-start.2 = ((bf16[8,16,8,128]{3,2,1,0:T(8,128)(2,1)}), bf16[8,16,8,128]{3,2,1,0:T(8,128)(2,1)}, u32[]{:S(2)}, u32[]{:S(2)}) async-start(bf16[8,16,8,128]{3,2,1,0:T(8,128)(2,1)} %param.8), calls=%async_computation.2 | async-start | bytes 524288 | tf_op jit(solution)/shard_map/all_to_all | solution.py:122
  250.1 14.8 %all-to-all-start.5 = ((bf16[8,16,8,128]{3,2,1,0:T(8,128)(2,1)}), bf16[8,16,8,128]{3,2,1,0:T(8,128)(2,1)}, u32[]{:S(2)}, u32[]{:S(2)}) async-start(bf16[8,16,8,128]{3,2,1,0:T(8,128)(2,1)} %param.11), calls=%async_computation.5 | async-start | bytes 524288 | tf_op jit(solution)/shard_map/all_to_all | solution.py:123
  397.4 15.9 %copy-start.133 = (f32[4,64,8]{1,2,0:T(8,128)S(1)}, f32[4,64,8]{1,2,0:T(8,128)}, u32[]{:S(2)}) copy-start(f32[4,64,8]{1,2,0:T(8,128)} %copy-done.132) | copy-start | bytes 24580
  399.8 8.4 %all-to-all-start.21 = ((bf16[64,2,8]{2,1,0:T(2,128)(2,1)}), bf16[64,2,8]{2,1,0:T(2,128)(2,1)S(1)}, u32[]{:S(2)}, u32[]{:S(2)}) async-start(bf16[64,2,8]{2,1,0:T(2,128)(2,1)} %add_convert_fusion), calls=%async_computation.21 | async-start | bytes 65536 | tf_op jit(solution)/shard_map/all_to_all | solution.py:138
  408.2 10.6 %all-to-all-start.18 = ((bf16[4,2,128]{2,1,0:T(2,128)(2,1)}), bf16[4,2,128]{2,1,0:T(2,128)(2,1)S(1)}, u32[]{:S(2)}, u32[]{:S(2)}) async-start(bf16[4,2,128]{2,1,0:T(2,128)(2,1)} %reshape.580), calls=%async_computation.18 | async-start | bytes 4096 | tf_op jit(solution)/shard_map/all_to_all | solution.py:127
  418.7 8.7 %all-to-all-start.20 = ((bf16[4,2,128]{2,1,0:T(2,128)(2,1)}), bf16[4,2,128]{2,1,0:T(2,128)(2,1)S(1)}, u32[]{:S(2)}, u32[]{:S(2)}) async-start(bf16[4,2,128]{2,1,0:T(2,128)(2,1)} %reshape.582), calls=%async_computation.20 | async-start | bytes 4096 | tf_op jit(solution)/shard_map/all_to_all | solution.py:127
  425.2 26.2 %copy-start.100 = (f32[4,64,8,128]{3,2,0,1:T(8,128)S(1)}, f32[4,64,8,128]{3,2,0,1:T(8,128)}, u32[]{:S(2)}) copy-start(f32[4,64,8,128]{3,2,0,1:T(8,128)} %copy-done.99) | copy-start | bytes 3145732
  425.2 26.2 %slice-start.1 = ((f32[4,64,8,128]{3,2,0,1:T(8,128)}), f32[2,64,8,128]{3,2,0,1:T(8,128)S(1)}, s32[]{:S(2)}) async-start(f32[4,64,8,128]{3,2,0,1:T(8,128)} %copy-done.99), calls=%async_computation.23 | async-start | bytes 1048576 | tf_op jit(solution)/shard_map/transpose(jvp())/split | solution.py:99
  427.4 10.3 %all-to-all-start.13 = ((bf16[64,2,8,128]{3,2,1,0:T(8,128)(2,1)}), bf16[64,2,8,128]{3,2,1,0:T(8,128)(2,1)S(1)}, u32[]{:S(2)}, u32[]{:S(2)}) async-start(bf16[64,2,8,128]{3,2,1,0:T(8,128)(2,1)} %fusion.87), calls=%async_computation.13 | async-start | bytes 524288 | tf_op jit(solution)/shard_map/all_to_all | solution.py:138
  437.7 10.3 %all-to-all-start.17 = ((bf16[64,2,8,128]{3,2,1,0:T(8,128)(2,1)}), bf16[64,2,8,128]{3,2,1,0:T(8,128)(2,1)S(1)}, u32[]{:S(2)}, u32[]{:S(2)}) async-start(bf16[64,2,8,128]{3,2,1,0:T(8,128)(2,1)} %fusion.89), calls=%async_computation.17 | async-start | bytes 524288 | tf_op jit(solution)/shard_map/all_to_all | solution.py:138
  441.1 20.6 %copy-start.136 = (f32[8,16,8]{1,2,0:T(8,128)S(1)}, f32[8,16,8]{1,2,0:T(8,128)}, u32[]{:S(2)}) copy-start(f32[8,16,8]{1,2,0:T(8,128)} %copy.1101) | copy-start | bytes 12292
  448.0 10.3 %all-to-all-start.15 = ((bf16[64,2,8,128]{3,2,1,0:T(8,128)(2,1)}), bf16[64,2,8,128]{3,2,1,0:T(8,128)(2,1)S(1)}, u32[]{:S(2)}, u32[]{:S(2)}) async-start(bf16[64,2,8,128]{3,2,1,0:T(8,128)(2,1)} %fusion.85), calls=%async_computation.15 | async-start | bytes 524288 | tf_op jit(solution)/shard_map/all_to_all | solution.py:138
  458.3 15.4 %copy-start.111 = (bf16[64,2,8,128]{3,2,1,0:T(8,128)(2,1)}, bf16[64,2,8,128]{3,2,1,0:T(8,128)(2,1)S(1)}, u32[]{:S(2)}) copy-start(bf16[64,2,8,128]{3,2,1,0:T(8,128)(2,1)S(1)} %all-to-all-done.15) | copy-start | bytes 786436
  458.3 11.9 %all-to-all-start.6 = ((bf16[2,64,8,128]{3,2,0,1:T(8,128)(2,1)}), bf16[2,64,8,128]{3,2,0,1:T(8,128)(2,1)S(1)}, u32[]{:S(2)}, u32[]{:S(2)}) async-start(bf16[2,64,8,128]{3,2,0,1:T(8,128)(2,1)} %fusion.88), calls=%async_computation.6 | async-start | bytes 524288 | tf_op jit(solution)/shard_map/all_to_all | solution.py:127
  470.1 10.3 %all-to-all-start.16 = ((bf16[2,64,8,128]{3,2,0,1:T(8,128)(2,1)}), bf16[2,64,8,128]{3,2,0,1:T(8,128)(2,1)S(1)}, u32[]{:S(2)}, u32[]{:S(2)}) async-start(bf16[2,64,8,128]{3,2,0,1:T(8,128)(2,1)} %fusion.84), calls=%async_computation.16 | async-start | bytes 524288 | tf_op jit(solution)/shard_map/all_to_all | solution.py:127
  480.5 10.2 %all-to-all-start.14 = ((bf16[2,64,8,128]{3,2,0,1:T(8,128)(2,1)}), bf16[2,64,8,128]{3,2,0,1:T(8,128)(2,1)S(1)}, u32[]{:S(2)}, u32[]{:S(2)}) async-start(bf16[2,64,8,128]{3,2,0,1:T(8,128)(2,1)} %fusion.86), calls=%async_computation.14 | async-start | bytes 524288 | tf_op jit(solution)/shard_map/all_to_all | solution.py:127
  (150 other events, 585.1 us)
where the time goes:
time: 499 us; the launch traced here: 493 us
  matrix products  207 us (41%)
  waiting for transfers between devices  86.2 us (17%)
  starting transfers between devices  84.1 us (17%)
  other arithmetic  58 us (12%)
  local copies, waits for them, and re-layouts  53.3 us (11%)
    dot_general x30, matrix products, advance(): power = jnp.einsum('btj,bjs->bts', power, power, precision=highest)  54.5 us
    dot_general x30, matrix products, advance(): jnp.einsum('btj,bjs->bts', power, inverse, precision=highest)  50.5 us
    all_to_all x5, waiting for transfers between devices, on_device(): lax.all_to_all(as_sent(pair_grads(arrived, 1)), 'gc', split_axis=1, conca...  26.9 us
    unnamed x330, local copies, waits for them, and re-layouts  19.5 us
    all_to_all x5, starting transfers between devices, on_device(): lax.all_to_all(as_sent(pair_grads(arrived, 1)), 'gc', split_axis=1, conca...  18.5 us
    all_to_all x5, waiting for transfers between devices, on_device(): lax.all_to_all(as_sent(pair_grads(arrived, 0)), 'gr', split_axis=0, conca...  18.3 us
    all_to_all x5, starting transfers between devices, on_device(): lax.all_to_all(as_sent(pair_grads(arrived, 0)), 'gr', split_axis=0, conca...  17.8 us
    dot_general x6, matrix products, advance(): writes = jnp.einsum('btj,bje->bte', inverse, right_side, precision=highest)  16.8 us
  transfers between devices with their start and end apart: 22, of which 19 were waited for; matrix products, arithmetic and copies ran while one was open for 13% of the time, Pallas kernels for 0%

commit v1 on v0

v1 whole, which is shorter than its diff:
```python
import functools

import jax
import jax.numpy as jnp
from jax import lax
from jax.experimental import pallas as pl
from jax.experimental.pallas import tpu as pltpu
from jax.sharding import PartitionSpec as P

bf16, f32 = jnp.bfloat16, jnp.float32
lanes = 128
together = 2


def dot(a, b):
    return lax.dot_general(
        a.astype(bf16), b.astype(bf16), (((1,), (0,)), ((), ())), preferred_element_type=f32
    )


def dot_t(a, b):
    return lax.dot_general(
        a.astype(bf16), b.astype(bf16), (((1,), (1,)), ((), ())), preferred_element_type=f32
    )


def unit_inverse(x, line, apart):
    u = jnp.where(apart == 1, -x, 0.0)
    size = 2
    while size < line:
        part = jnp.where((apart >= size) & (apart < 2 * size), x, 0.0)
        left = part + dot(u, part)
        u = u - (left + dot(left, u))
        size *= 2
    return u


def solve(q, k, v, o, beta_r, decay_r, line):
    i = lax.broadcasted_iota(jnp.int32, (lanes, lanes), 0)
    j = lax.broadcasted_iota(jnp.int32, (lanes, lanes), 1)
    apart = i ^ j
    same = apart < line
    eye = apart == 0
    low, up = same & (i > j), same & (i < j)
    upto, since = same & (i >= j), same & (i <= j)
    low_m, up_m = jnp.where(low, 1.0, 0.0), jnp.where(up, 1.0, 0.0)
    upto_m, since_m = jnp.where(upto, 1.0, 0.0), jnp.where(since, 1.0, 0.0)

    kk0, qk0, kq0 = dot_t(k, k), dot_t(q, k), dot_t(k, q)
    y, yt = dot_t(o, v), dot_t(v, o)
    qf, kf = q.astype(f32), k.astype(f32)
    rq = lax.rsqrt(jnp.sum(qf * qf, axis=1, keepdims=True) + 1e-6)
    rk = lax.rsqrt(jnp.sum(kf * kf, axis=1, keepdims=True) + 1e-6)
    rq_r = jnp.sum(jnp.where(eye, rq, 0.0), axis=0, keepdims=True)
    rk_r = jnp.sum(jnp.where(eye, rk, 0.0), axis=0, keepdims=True)
    beta = dot(jnp.where(eye, beta_r, 0.0), jnp.ones((lanes, lanes), f32))
    gap = dot(jnp.where(upto, decay_r, 0.0), low_m) + dot(jnp.where(since, decay_r, 0.0), up_m)
    gap_t = dot(jnp.where(low, decay_r, 0.0), upto_m) + dot(jnp.where(up, decay_r, 0.0), since_m)
    h = jnp.where(same, jnp.exp(-gap), 0.0)
    ht = jnp.where(same, jnp.exp(-gap_t), 0.0)

    kk = kk0 * rk * rk_r
    x = kk * ht * beta_r
    uf = unit_inverse(jnp.where(up, x, 0.0), line, apart)
    ub = unit_inverse(jnp.where(low, x, 0.0), line, apart)
    pt = kq0 * rk * rq_r * ht
    ptf, ptb = jnp.where(low, 0.0, pt), jnp.where(up, 0.0, pt)
    mtf = ptf + dot(uf, ptf)
    mtb = ptb + dot(ub, ptb)
    yb = y * beta_r
    zf = yb + dot(yb, uf)
    zb = yb + dot(yb, ub)
    da = -jnp.where(low, dot(mtf, zf), jnp.where(up, dot(mtb, zb), 0.0))
    dp = jnp.where(low, zf, jnp.where(up, zb, zf + zb))
    ds = dp * h
    n1 = da * h
    n1k = n1 * kk
    n = n1 * beta
    e = ds * (qk0 * rq * rk_r) + n1k * beta
    mt = mtf + mtb
    dbeta = dot_t(jnp.ones((16, lanes), f32), n1k + mt * yt)[0:1]
    behind = jnp.where(upto, dot(jnp.where(low, e, 0.0), up_m), 0.0)
    ahead = jnp.where(since, dot(jnp.where(up, e, 0.0), low_m), 0.0)
    ddecay = -jnp.sum(behind + ahead, axis=0, keepdims=True)
    dv = beta * dot(mt, o)
    dqn = dot(ds * rk_r, k)
    dq = rq * (dqn - qf * (rq * rq * jnp.sum(dqn * qf, axis=1, keepdims=True)))
    dkn = dot(jnp.transpose(ds * rq), q) + dot((n + jnp.transpose(n)) * rk_r, k)
    dk = rk * (dkn - kf * (rk * rk * jnp.sum(dkn * kf, axis=1, keepdims=True)))
    return (dq, dk, dv), dbeta, ddecay


class Phase:
    def __init__(self, axis, count, heads, source, gains, back, gains_back, scratch):
        self.axis, self.count, self.heads = axis, count, heads
        self.source, self.gains, self.back, self.gains_back = source, gains, back, gains_back
        (self.held, self.gains_held, self.result, self.sums, self.gains_result, self.send,
         self.recv, self.own, self.back_send, self.back_recv, self.back_own) = scratch
        self.lines = self.held.shape[1]
        self.span = self.held.shape[3]
        self.tokens = count * self.span // heads
        self.me = lax.axis_index(axis)
        self.problems = self.lines * self.tokens * heads // lanes // self.lines

    def to(self, step):
        return lax.rem(self.me + step, self.count)

    def out_copies(self, line):
        copies = []
        for step in range(self.count):
            to = self.to(step)
            if line < self.lines:
                src, dst = self.source.at[to * self.lines + line], self.held.at[self.me, line]
            else:
                src, dst = self.gains.at[to], self.gains_held.at[self.me]
            copies.append(self.copy(src, dst, step, line, to, self.send, self.recv, self.own))
        return copies

    def back_copies(self, line):
        copies = []
        for step in range(self.count):
            to = self.to(step)
            if line < self.lines:
                src, dst = self.result.at[to, line], self.back.at[self.me * self.lines + line]
            else:
                src, dst = self.gains_result, self.gains_back.at[self.me]
            copies.append(
                self.copy(src, dst, step, line, to, self.back_send, self.back_recv, self.back_own)
            )
        return copies

    def copy(self, src, dst, step, line, to, send, recv, own):
        if step == 0:
            return pltpu.make_async_copy(src, dst, own.at[line])
        return pltpu.make_async_remote_copy(
            src_ref=src,
            dst_ref=dst,
            send_sem=send.at[line, step - 1],
            recv_sem=recv.at[line, step - 1],
            device_id={self.axis: to},
            device_id_type=pl.DeviceIdType.MESH,
        )

    def solve_line(self, line, stage, grads):
        tokens, heads, span = self.tokens, self.heads, self.span
        total = tokens * heads
        for member in range(4):
            for peer in range(self.count):
                stage[pl.ds(member * total + peer * span, span), :] = self.held[
                    peer, line, member
                ].astype(f32)
        joined = lanes // tokens
        half = self.gains_held.shape[1] // 2
        gains = self.gains_held[0].astype(f32)
        for peer in range(1, self.count):
            gains = gains + self.gains_held[peer].astype(f32)
        if line == 0:
            self.sums[...] = gains

        def some(index, carry):
            for extra in range(together):
                group = index * together + extra
                row = line * self.problems + group

                def fetch(member):
                    parts = [
                        stage[pl.ds(member * total + group * joined + part, tokens, stride=heads), :]
                        for part in range(joined)
                    ]
                    return jnp.concatenate(parts, axis=0).astype(bf16)

                found, dbeta, ddecay = solve(
                    fetch(0), fetch(1), fetch(2), fetch(3),
                    self.sums[pl.ds(row, 1), :], self.sums[pl.ds(half + row, 1), :], tokens,
                )
                for member in range(3):
                    for part in range(joined):
                        place = pl.ds(member * total + group * joined + part, tokens, stride=heads)
                        grads[place, :] = found[member][part * tokens : (part + 1) * tokens]
                self.sums[pl.ds(row, 1), :] = dbeta
                self.sums[pl.ds(half + row, 1), :] = ddecay
            return carry

        lax.fori_loop(0, self.problems // together, some, 0)
        for member in range(3):
            for peer in range(self.count):
                self.result[peer, line, member] = grads[
                    pl.ds(member * total + peer * span, span), :
                ].astype(bf16)


def kernel(counts, heads, *refs):
    ins, outs, scratch = refs[:4], refs[4:8], refs[8:]
    each = (len(scratch) - 2) // 2
    stage, grads = scratch[-2:]
    row = Phase("gc", counts[0], heads, ins[0], ins[1], outs[0], outs[1], scratch[:each])
    column = Phase("gr", counts[1], heads, ins[2], ins[3], outs[2], outs[3], scratch[each:-2])

    barrier = pltpu.get_barrier_semaphore()
    for phase in (row, column):
        for step in range(1, phase.count):
            pl.semaphore_signal(
                barrier, inc=1, device_id={phase.axis: phase.to(step)},
                device_id_type=pl.DeviceIdType.MESH,
            )
    pl.semaphore_wait(barrier, row.count + column.count - 2)

    started = []

    def start(copies):
        for copy in copies[1:] + copies[:1]:
            copy.start()
        started.extend(copies[1:])
        return copies

    def arrive(copies):
        for copy in copies[1:]:
            copy.wait_recv()
        copies[0].wait()

    arriving = {}
    for phase in (row, column):
        arriving[phase.axis, phase.lines] = start(phase.out_copies(phase.lines))
    for phase in (row, column):
        for line in range(phase.lines):
            arriving[phase.axis, line] = start(phase.out_copies(line))

    returning = []
    for phase in (column, row):
        arrive(arriving[phase.axis, phase.lines])
        for line in range(phase.lines):
            arrive(arriving[phase.axis, line])
            phase.solve_line(line, stage, grads)
            returning.append(start(phase.back_copies(line)))
        phase.gains_result[...] = phase.sums[...].astype(bf16)
        returning.append(start(phase.back_copies(phase.lines)))
    for copies in returning:
        arrive(copies)
    for copy in started:
        copy.wait_send()


def spread(gains, count, own, tokens, joined):
    kinds, lines, span, heads = gains.shape
    shaped = gains.reshape(kinds, count, lines // count, span, heads // joined, joined)
    shaped = jnp.transpose(shaped, (1, 0, 2, 4, 5, 3))
    mine = (jnp.arange(count) == own)[:, None]
    placed = jnp.where(mine, shaped[..., None, :], jnp.zeros((), gains.dtype))
    return placed.reshape(count, -1, lanes)


def gather(gains, count, own, lines, span, heads, joined):
    shaped = gains.reshape(count, 2, lines // count, heads // joined, joined, count, span)
    mine = (jnp.arange(count) == own)[:, None]
    picked = jnp.sum(jnp.where(mine, shaped.astype(f32), 0.0), axis=5)
    return jnp.transpose(picked, (1, 0, 2, 5, 3, 4)).reshape(2, lines, span, heads)


def on_device(counts, queries, key_vectors, values, strength, decay_rate, out_grad):
    n_row, n_col = counts
    rows, cols, heads, size = queries.shape
    row_tokens, col_tokens = n_row * cols, n_col * rows
    row_joined, col_joined = lanes // row_tokens, lanes // col_tokens
    members = jnp.stack([queries, key_vectors, values, out_grad], axis=1)
    row_source = members.reshape(rows, 4, cols * heads, size)
    members = jnp.stack([queries, key_vectors, values, out_grad], axis=0)
    col_source = jnp.transpose(members, (2, 0, 1, 3, 4)).reshape(cols, 4, rows * heads, size)
    gains = jnp.stack([strength, decay_rate])
    row_own, col_own = lax.axis_index("gc"), lax.axis_index("gr")
    row_gains = spread(gains, n_row, row_own, row_tokens, row_joined)
    col_gains = spread(jnp.swapaxes(gains, 1, 2), n_col, col_own, col_tokens, col_joined)

    def scratch(count, lines, span, gains_rows):
        table = (gains_rows, lanes)
        sems = pltpu.SemaphoreType.DMA
        return [
            pltpu.VMEM((count, lines, 4, span, size), bf16),
            pltpu.VMEM((count,) + table, bf16),
            pltpu.VMEM((count, lines, 3, span, size), bf16),
            pltpu.VMEM(table, f32),
            pltpu.VMEM(table, bf16),
            sems((lines + 1, count - 1)),
            sems((lines + 1, count - 1)),
            sems((lines + 1,)),
            sems((lines + 1, count - 1)),
            sems((lines + 1, count - 1)),
            sems((lines + 1,)),
        ]

    most = max(row_tokens, col_tokens) * heads
    shapes = [
        jax.ShapeDtypeStruct((rows, 3, cols * heads, size), bf16),
        jax.ShapeDtypeStruct(row_gains.shape, bf16),
        jax.ShapeDtypeStruct((cols, 3, rows * heads, size), bf16),
        jax.ShapeDtypeStruct(col_gains.shape, bf16),
    ]
    row_back, row_gains_back, col_back, col_gains_back = pl.pallas_call(
        functools.partial(kernel, counts, heads),
        out_shape=shapes,
        in_specs=[pl.BlockSpec(memory_space=pl.ANY)] * 4,
        out_specs=[pl.BlockSpec(memory_space=pl.ANY)] * 4,
        scratch_shapes=scratch(n_row, rows // n_row, cols * heads, row_gains.shape[1])
        + scratch(n_col, cols // n_col, rows * heads, col_gains.shape[1])
        + [pltpu.VMEM((4 * most, size), f32), pltpu.VMEM((3 * most, size), f32)],
        compiler_params=pltpu.CompilerParams(
            collective_id=0, has_side_effects=True, vmem_limit_bytes=40 * 2**20
        ),
        name="exchange_and_solve",
    )(row_source, row_gains, col_source, col_gains)

    row_back = row_back.reshape(rows, 3, cols, heads, size)
    col_back = col_back.reshape(cols, 3, rows, heads, size)

    def merged(member):
        first = row_back[:, member].astype(f32)
        second = jnp.swapaxes(col_back[:, member], 0, 1).astype(f32)
        return (first + second).astype(bf16)

    row_small = gather(row_gains_back, n_row, row_own, rows, cols, heads, row_joined)
    col_small = gather(col_gains_back, n_col, col_own, cols, rows, heads, col_joined)
    small = (row_small + jnp.swapaxes(col_small, 1, 2)).astype(bf16)
    return (merged(0), merged(1), merged(2), small[0], small[1])


def solution(mesh):
    counts = (mesh.shape["gc"], mesh.shape["gr"])
    wide = P("gr", "gc", None, None)
    narrow = P("gr", "gc", None)
    return jax.shard_map(
        functools.partial(on_device, counts),
        mesh=mesh,
        in_specs=(wide, wide, wide, narrow, narrow, wide),
        out_specs=(wide, wide, wide, narrow, narrow),
        check_vma=False,
    )
```

time: 499 us -> 79.5 us (0.16); the launches traced: 493 us -> 78.4 us
  matrix products: 207 us -> 0 us
  waiting for transfers between devices: 86.2 us -> 0 us
  starting transfers between devices: 84.1 us -> 0 us
  Pallas kernels: 0 us -> 71.5 us
  other arithmetic: 58 us -> 2.27 us
  local copies, waits for them, and re-layouts: 53.3 us -> 3.89 us
    dot_general x94 -> x0, matrix products: 207 us -> none  [the longest x30 54.5 us: advance(): power = jnp.einsum('btj,bjs->bts', power, power, precision=highest)]
    all_to_all x22 -> x0, waiting for transfers between devices: 86.2 us -> none  [the longest x5 26.9 us: on_device(): lax.all_to_all(as_sent(pair_grads(arrived, 1)), 'gc', split_axis=1, conca...]
    all_to_all x22 -> x0, starting transfers between devices: 84.1 us -> none  [the longest x5 18.5 us: on_device(): lax.all_to_all(as_sent(pair_grads(arrived, 1)), 'gc', split_axis=1, conca...]
    pallas_call x0 -> x1, Pallas kernels: none -> 71.5 us  [on_device(): pl.pallas_call(functools.partial(kernel, counts, heads), out_shape=shapes...]
    unnamed x330 -> x14, local copies, waits for them, and re-layouts: 19.5 us -> 1.12 us
    convert_element_type x28 -> x2, other arithmetic: 15.7 us -> 1.03 us  [the longest x1 1.02 us: merged(): return (first + second).astype(bf16)]
    add_any x6 -> x0, other arithmetic: 11.9 us -> none  [the longest x4 8.48 us: normalize(): tensor * tensor]
    reduce_sum x9 -> x2, other arithmetic: 10.7 us -> 0.72 us  [gather(): picked = jnp.sum(jnp.where(mine, shaped.astype(f32), 0.0), axis=5)]
  transfers between devices with their start and end apart: 22 -> 0, of which waited for: 19 -> 0; matrix products, arithmetic and copies ran while one was open for 13% -> 0% of each run, Pallas kernels for 0% -> 0%
where the time goes in v1:
time: 79.5 us; the launch traced here: 78.4 us
  Pallas kernels  71.5 us (90%)
  local copies, waits for them, and re-layouts  3.89 us (5%)
  other arithmetic  2.27 us (3%)
  between operations  0.84 us (1%)
    pallas_call x1, Pallas kernels, on_device(): pl.pallas_call(functools.partial(kernel, counts, heads), out_shape=shapes...  71.5 us

profile of v1, /device:TPU:0, one launch (start us, length us, event | category | flops | bytes accessed | tf_op | source)
XLA Modules:
  0.0 78.4 jit_solution(12670376762133365407)
XLA Ops:
  0.6 0.0 copy-start.5
  0.7 0.1 broadcast_in_dim.82
  0.8 0.1 broadcast_in_dim.83
  0.8 0.1 broadcast_in_dim.88
  0.9 0.1 broadcast_in_dim.89
  1.0 0.3 copy-done.5
  1.4 0.0 copy-done.4
  1.4 0.1 maximum_bitcast_fusion.1
  1.5 0.1 copy.47
  1.6 0.1 copy.48
  1.8 0.1 broadcast_in_dim.86
  2.0 0.0 copy-start.2
  2.0 0.0 copy-start.3
  2.0 0.1 broadcast_in_dim.91
  2.1 0.0 copy-start
  2.1 0.0 copy-start.1
  2.1 0.5 broadcast_in_dim.92
  2.7 0.3 copy-done.2
  2.9 0.1 copy-done.3
  3.0 0.1 copy-done
  3.1 0.1 copy-done.1
  3.2 0.1 pad_maximum_fusion.refs_0_
  3.3 0.3 copy_bitcast_fusion.refs_2_
  3.6 71.5 %exchange_and_solve.1 = (bf16[8,3,128,128]{3,2,1,0:T(8,128)(2,1)S(1)}, bf16[4,16,128]{2,1,0:T(8,128)(2,1)S(1)}, bf16[16,3,64,128]{3,2,1,0:T(8,128)(2,1)S(1)}, bf16[8,16,128]{2,1,0:T(8,128)(2,1)S(1)}) custom-call(bf16[8,4,128,128]{3,2,1,0:T(8,128)(2,1)S(1)} %pad_maximum_fusion.refs_0_, bf16[4,16,128]{2,1,0:T(8,128)(2,1)S(1)} %broadcast_select_fusion.1.refs_1_, ...), custom_call_target="tpu_custom_call" | custom-call | tf_op jit(solution)/shard_map/exchange_and_solve/pallas_call | solution.py:297
  75.1 0.1 fusion.7
  75.1 1.0 %fusion.1 = (bf16[8,16,8,128]{3,2,1,0:T(8,128)(2,1)}, bf16[8,16,8,128]{3,2,1,0:T(8,128)(2,1)}, bf16[8,16,8,128]{3,2,1,0:T(8,128)(2,1)}) fusion(bf16[8,3,16,8,128]{4,3,2,1,0:T(8,128)(2,1)S(1)} %bitcast.95, bf16[16,1,8,8,128]{4,3,2,1,0:T(8,128)(2,1)S(1)} %get-tuple-element.21, bf16[16,1,8,8,128]{4,3,2,1,0:T(8,128)(2,1)S(1)} %get-tuple-element.22, ...), kind=kLoop, calls=%fused_computation.6 | loop fusion | flops 1572864 | bytes 2359296 | tf_op jit(solution)/shard_map/convert_element_type | solution.py:317
  76.2 0.2 reshape.77
  76.4 0.3 select_reduce_fusion.1
  76.7 0.5 reshape.78
  77.2 0.4 select_reduce_fusion
  77.7 0.1 copy.58
  77.8 0.6 slice_bitcast_fusion.3
  (12 shorter events, 0.2 us)
Async XLA Ops:
  0.6 0.7 copy-start.5
  0.6 0.7 copy-start.4
  2.0 1.0 %copy-start.2 = (bf16[8,16,8,128]{3,2,1,0:T(8,128)(2,1)S(1)}, bf16[8,16,8,128]{3,2,1,0:T(8,128)(2,1)}, u32[]{:S(2)}) copy-start(bf16[8,16,8,128]{3,2,1,0:T(8,128)(2,1)} %param.7) | copy-start | bytes 786436
  2.0 1.0 %copy-start.3 = (bf16[8,16,8,128]{3,2,1,0:T(8,128)(2,1)S(1)}, bf16[8,16,8,128]{3,2,1,0:T(8,128)(2,1)}, u32[]{:S(2)}) copy-start(bf16[8,16,8,128]{3,2,1,0:T(8,128)(2,1)} %param.6) | copy-start | bytes 786436
  2.1 1.0 %copy-start = (bf16[8,16,8,128]{3,2,1,0:T(8,128)(2,1)S(1)}, bf16[8,16,8,128]{3,2,1,0:T(8,128)(2,1)}, u32[]{:S(2)}) copy-start(bf16[8,16,8,128]{3,2,1,0:T(8,128)(2,1)} %param.11) | copy-start | bytes 786436
  2.1 1.1 %copy-start.1 = (bf16[8,16,8,128]{3,2,1,0:T(8,128)(2,1)S(1)}, bf16[8,16,8,128]{3,2,1,0:T(8,128)(2,1)}, u32[]{:S(2)}) copy-start(bf16[8,16,8,128]{3,2,1,0:T(8,128)(2,1)} %param.8) | copy-start | bytes 786436

commit v2 on v1

--- a/solution.py
+++ b/solution.py
@@ -9,7 +9,7 @@
 
 bf16, f32 = jnp.bfloat16, jnp.float32
 lanes = 128
-together = 2
+together = 4
 
 
 def dot(a, b):
@@ -24,70 +24,102 @@
     )
 
 
-def unit_inverse(x, line, apart):
-    u = jnp.where(apart == 1, -x, 0.0)
+class Masks:
+    def __init__(self, line):
+        i = lax.broadcasted_iota(jnp.int32, (lanes, lanes), 0)
+        j = lax.broadcasted_iota(jnp.int32, (lanes, lanes), 1)
+        self.line, self.apart = line, i ^ j
+        self.same = self.apart < line
+        self.eye = self.apart == 0
+        self.low, self.up = self.same & (i > j), self.same & (i < j)
+        self.upto, self.since = self.same & (i >= j), self.same & (i <= j)
+        names = ("low", "up", "upto", "since")
+        self.ones = {
+            name: jnp.where(getattr(self, name), 1.0, 0.0).astype(bf16) for name in names
+        }
+
+
+def unit_inverses(xs, masks):
+    us = [jnp.where(masks.apart == 1, -x, 0.0) for x in xs]
     size = 2
-    while size < line:
-        part = jnp.where((apart >= size) & (apart < 2 * size), x, 0.0)
-        left = part + dot(u, part)
-        u = u - (left + dot(left, u))
+    while size < masks.line:
+        here = (masks.apart >= size) & (masks.apart < 2 * size)
+        parts = [jnp.where(here, x, 0.0) for x in xs]
+        lefts = [part + dot(u, part) for u, part in zip(us, parts)]
+        yield
+        us = [u - (left + dot(left, u)) for u, left in zip(us, lefts)]
+        yield
         size *= 2
-    return u
-
-
-def solve(q, k, v, o, beta_r, decay_r, line):
-    i = lax.broadcasted_iota(jnp.int32, (lanes, lanes), 0)
-    j = lax.broadcasted_iota(jnp.int32, (lanes, lanes), 1)
-    apart = i ^ j
-    same = apart < line
-    eye = apart == 0
-    low, up = same & (i > j), same & (i < j)
-    upto, since = same & (i >= j), same & (i <= j)
-    low_m, up_m = jnp.where(low, 1.0, 0.0), jnp.where(up, 1.0, 0.0)
-    upto_m, since_m = jnp.where(upto, 1.0, 0.0), jnp.where(since, 1.0, 0.0)
-
-    kk0, qk0, kq0 = dot_t(k, k), dot_t(q, k), dot_t(k, q)
-    y, yt = dot_t(o, v), dot_t(v, o)
+    return us
+
+
+def solve(q, k, v, o, beta_r, decay_r, masks):
+    eye, low, up, same = masks.eye, masks.low, masks.up, masks.same
+    upto, since, ones = masks.upto, masks.since, masks.ones
+    kk0, kq0 = dot_t(k, k), dot_t(k, q)
     qf, kf = q.astype(f32), k.astype(f32)
     rq = lax.rsqrt(jnp.sum(qf * qf, axis=1, keepdims=True) + 1e-6)
     rk = lax.rsqrt(jnp.sum(kf * kf, axis=1, keepdims=True) + 1e-6)
     rq_r = jnp.sum(jnp.where(eye, rq, 0.0), axis=0, keepdims=True)
     rk_r = jnp.sum(jnp.where(eye, rk, 0.0), axis=0, keepdims=True)
-    beta = dot(jnp.where(eye, beta_r, 0.0), jnp.ones((lanes, lanes), f32))
-    gap = dot(jnp.where(upto, decay_r, 0.0), low_m) + dot(jnp.where(since, decay_r, 0.0), up_m)
-    gap_t = dot(jnp.where(low, decay_r, 0.0), upto_m) + dot(jnp.where(up, decay_r, 0.0), since_m)
-    h = jnp.where(same, jnp.exp(-gap), 0.0)
+    gap_t = dot(jnp.where(low, decay_r, 0.0), ones["upto"])
+    gap_t = gap_t + dot(jnp.where(up, decay_r, 0.0), ones["since"])
+    yield
     ht = jnp.where(same, jnp.exp(-gap_t), 0.0)
-
     kk = kk0 * rk * rk_r
     x = kk * ht * beta_r
-    uf = unit_inverse(jnp.where(up, x, 0.0), line, apart)
-    ub = unit_inverse(jnp.where(low, x, 0.0), line, apart)
+    uf, ub = yield from unit_inverses(
+        [jnp.where(up, x, 0.0), jnp.where(low, x, 0.0)], masks
+    )
+    y = dot_t(o, v)
     pt = kq0 * rk * rq_r * ht
     ptf, ptb = jnp.where(low, 0.0, pt), jnp.where(up, 0.0, pt)
     mtf = ptf + dot(uf, ptf)
     mtb = ptb + dot(ub, ptb)
+    yield
     yb = y * beta_r
     zf = yb + dot(yb, uf)
     zb = yb + dot(yb, ub)
-    da = -jnp.where(low, dot(mtf, zf), jnp.where(up, dot(mtb, zb), 0.0))
+    gap = dot(jnp.where(upto, decay_r, 0.0), ones["low"])
+    gap = gap + dot(jnp.where(since, decay_r, 0.0), ones["up"])
+    yield
     dp = jnp.where(low, zf, jnp.where(up, zb, zf + zb))
+    h = jnp.where(same, jnp.exp(-gap), 0.0)
+    daf, dab = dot(mtf, zf), dot(mtb, zb)
+    beta = dot(jnp.where(eye, beta_r, 0.0), jnp.ones((lanes, lanes), bf16))
+    qk0, yt = dot_t(q, k), dot_t(v, o)
+    mt = mtf + mtb
+    dv = beta * dot(mt, o)
     ds = dp * h
-    n1 = da * h
+    dqn = dot(ds * rk_r, k)
+    yield
+    n1 = jnp.where(low, daf, jnp.where(up, dab, 0.0)) * -h
     n1k = n1 * kk
     n = n1 * beta
     e = ds * (qk0 * rq * rk_r) + n1k * beta
-    mt = mtf + mtb
-    dbeta = dot_t(jnp.ones((16, lanes), f32), n1k + mt * yt)[0:1]
-    behind = jnp.where(upto, dot(jnp.where(low, e, 0.0), up_m), 0.0)
-    ahead = jnp.where(since, dot(jnp.where(up, e, 0.0), low_m), 0.0)
-    ddecay = -jnp.sum(behind + ahead, axis=0, keepdims=True)
-    dv = beta * dot(mt, o)
-    dqn = dot(ds * rk_r, k)
+    dbeta = dot_t(jnp.ones((16, lanes), bf16), n1k + mt * yt)[0:1]
+    behind = dot(jnp.where(low, e, 0.0), ones["up"])
+    ahead = dot(jnp.where(up, e, 0.0), ones["low"])
+    dkn = dot(jnp.transpose(ds * rq), q) + dot((n + jnp.transpose(n)) * rk_r, k)
+    yield
+    ddecay = jnp.where(upto, behind, 0.0) + jnp.where(since, ahead, 0.0)
+    ddecay = -jnp.sum(ddecay, axis=0, keepdims=True)
     dq = rq * (dqn - qf * (rq * rq * jnp.sum(dqn * qf, axis=1, keepdims=True)))
-    dkn = dot(jnp.transpose(ds * rq), q) + dot((n + jnp.transpose(n)) * rk_r, k)
     dk = rk * (dkn - kf * (rk * rk * jnp.sum(dkn * kf, axis=1, keepdims=True)))
     return (dq, dk, dv), dbeta, ddecay
+
+
+def abreast(generators):
+    results = [None] * len(generators)
+    waiting = list(range(len(generators)))
+    while waiting:
+        for index in list(waiting):
+            try:
+                next(generators[index])
+            except StopIteration as stop:
+                results[index] = stop.value
+                waiting.remove(index)
+    return results
 
 
 class Phase:
@@ -157,22 +189,25 @@
         if line == 0:
             self.sums[...] = gains
 
+        def fetch(group, member):
+            parts = [
+                stage[pl.ds(member * total + group * joined + part, tokens, stride=heads), :]
+                for part in range(joined)
+            ]
+            return jnp.concatenate(parts, axis=0).astype(bf16)
+
         def some(index, carry):
-            for extra in range(together):
-                group = index * together + extra
-                row = line * self.problems + group
-
-                def fetch(member):
-                    parts = [
-                        stage[pl.ds(member * total + group * joined + part, tokens, stride=heads), :]
-                        for part in range(joined)
-                    ]
-                    return jnp.concatenate(parts, axis=0).astype(bf16)
-
-                found, dbeta, ddecay = solve(
-                    fetch(0), fetch(1), fetch(2), fetch(3),
-                    self.sums[pl.ds(row, 1), :], self.sums[pl.ds(half + row, 1), :], tokens,
+            masks = Masks(tokens)
+            groups = [index * together + extra for extra in range(together)]
+            rows = [line * self.problems + group for group in groups]
+            solving = [
+                solve(
+                    *(fetch(group, member) for member in range(4)),
+                    self.sums[pl.ds(row, 1), :], self.sums[pl.ds(half + row, 1), :], masks,
                 )
+                for group, row in zip(groups, rows)
+            ]
+            for group, row, (found, dbeta, ddecay) in zip(groups, rows, abreast(solving)):
                 for member in range(3):
                     for part in range(joined):
                         place = pl.ds(member * total + group * joined + part, tokens, stride=heads)
@@ -228,12 +263,16 @@
     returning = []
     for phase in (column, row):
         arrive(arriving[phase.axis, phase.lines])
-        for line in range(phase.lines):
+    for line in range(max(row.lines, column.lines)):
+        for phase in (column, row):
+            if line >= phase.lines:
+                continue
             arrive(arriving[phase.axis, line])
             phase.solve_line(line, stage, grads)
             returning.append(start(phase.back_copies(line)))
-        phase.gains_result[...] = phase.sums[...].astype(bf16)
-        returning.append(start(phase.back_copies(phase.lines)))
+            if line == phase.lines - 1:
+                phase.gains_result[...] = phase.sums[...].astype(bf16)
+                returning.append(start(phase.back_copies(phase.lines)))
     for copies in returning:
         arrive(copies)
     for copy in started:

time: 79.5 us -> 56.3 us (0.71)
  Pallas kernels: 71.5 us -> 48.9 us
    pallas_call x1, Pallas kernels: 71.5 us -> 48.9 us  [on_device(): pl.pallas_call(functools.partial(kernel, counts, heads), out_shape=shapes...]
where the time goes in v2:
time: 56.3 us; the launch traced here: 55.9 us
  Pallas kernels  48.9 us (87%)
  local copies, waits for them, and re-layouts  3.89 us (7%)
  other arithmetic  2.27 us (4%)
  between operations  0.84 us (1%)
    pallas_call x1, Pallas kernels, on_device(): pl.pallas_call(functools.partial(kernel, counts, heads), out_shape=shapes...  48.9 us
    broadcast_in_dim x8, local copies, waits for them, and re-layouts, spread(): placed = jnp.where(mine, shaped[..., None, :], jnp.zeros((), gains.dtype))  1.13 us

profile of v2, /device:TPU:0, one launch (start us, length us, event | category | flops | bytes accessed | tf_op | source)
XLA Modules:
  0.0 55.9 jit_solution(6861870244213089451)
XLA Ops:
  0.6 0.0 copy-start.5
  0.7 0.1 broadcast_in_dim.82
  0.8 0.1 broadcast_in_dim.83
  0.8 0.1 broadcast_in_dim.88
  0.9 0.1 broadcast_in_dim.89
  1.0 0.3 copy-done.5
  1.4 0.0 copy-done.4
  1.4 0.1 maximum_bitcast_fusion.1
  1.5 0.1 copy.47
  1.6 0.1 copy.48
  1.8 0.1 broadcast_in_dim.86
  2.0 0.0 copy-start.2
  2.0 0.0 copy-start.3
  2.0 0.1 broadcast_in_dim.91
  2.1 0.0 copy-start
  2.1 0.0 copy-start.1
  2.1 0.5 broadcast_in_dim.92
  2.7 0.3 copy-done.2
  2.9 0.1 copy-done.3
  3.0 0.1 copy-done
  3.1 0.1 copy-done.1
  3.2 0.1 pad_maximum_fusion.refs_0_
  3.3 0.3 copy_bitcast_fusion.refs_2_
  3.6 48.9 %exchange_and_solve.1 = (bf16[8,3,128,128]{3,2,1,0:T(8,128)(2,1)S(1)}, bf16[4,16,128]{2,1,0:T(8,128)(2,1)S(1)}, bf16[16,3,64,128]{3,2,1,0:T(8,128)(2,1)S(1)}, bf16[8,16,128]{2,1,0:T(8,128)(2,1)S(1)}) custom-call(bf16[8,4,128,128]{3,2,1,0:T(8,128)(2,1)S(1)} %pad_maximum_fusion.refs_0_, bf16[4,16,128]{2,1,0:T(8,128)(2,1)S(1)} %broadcast_select_fusion.1.refs_1_, ...), custom_call_target="tpu_custom_call" | custom-call | tf_op jit(solution)/shard_map/exchange_and_solve/pallas_call | solution.py:336
  52.5 0.1 fusion.7
  52.6 1.0 %fusion.1 = (bf16[8,16,8,128]{3,2,1,0:T(8,128)(2,1)}, bf16[8,16,8,128]{3,2,1,0:T(8,128)(2,1)}, bf16[8,16,8,128]{3,2,1,0:T(8,128)(2,1)}) fusion(bf16[8,3,16,8,128]{4,3,2,1,0:T(8,128)(2,1)S(1)} %bitcast.95, bf16[16,1,8,8,128]{4,3,2,1,0:T(8,128)(2,1)S(1)} %get-tuple-element.21, bf16[16,1,8,8,128]{4,3,2,1,0:T(8,128)(2,1)S(1)} %get-tuple-element.22, ...), kind=kLoop, calls=%fused_computation.6 | loop fusion | flops 1572864 | bytes 2359296 | tf_op jit(solution)/shard_map/convert_element_type | solution.py:356
  53.6 0.2 reshape.77
  53.8 0.3 select_reduce_fusion.1
  54.1 0.5 reshape.78
  54.7 0.4 select_reduce_fusion
  55.2 0.1 copy.58
  55.3 0.6 %slice_bitcast_fusion.3 = (bf16[8,16,8]{1,2,0:T(8,128)(2,1)}, bf16[8,16,8]{1,2,0:T(8,128)(2,1)}) fusion(bf16[2,8,16,8]{2,3,1,0:T(8,128)(2,1)S(1)} %fusion.6), kind=kLoop, calls=%fused_computation.25 | loop fusion | bytes 8192 | tf_op jit(solution)/shard_map/squeeze | solution.py:361
  (12 shorter events, 0.2 us)
Async XLA Ops:
  0.6 0.7 %copy-start.5 = (bf16[8,16,8]{1,2,0:T(8,128)(2,1)S(1)}, bf16[8,16,8]{1,2,0:T(8,128)(2,1)}, u32[]{:S(2)}) copy-start(bf16[8,16,8]{1,2,0:T(8,128)(2,1)} %param.10) | copy-start | bytes 6148
  0.6 0.7 %copy-start.4 = (bf16[8,16,8]{1,2,0:T(8,128)(2,1)S(1)}, bf16[8,16,8]{1,2,0:T(8,128)(2,1)}, u32[]{:S(2)}) copy-start(bf16[8,16,8]{1,2,0:T(8,128)(2,1)} %param.9) | copy-start | bytes 6148
  2.0 1.0 %copy-start.2 = (bf16[8,16,8,128]{3,2,1,0:T(8,128)(2,1)S(1)}, bf16[8,16,8,128]{3,2,1,0:T(8,128)(2,1)}, u32[]{:S(2)}) copy-start(bf16[8,16,8,128]{3,2,1,0:T(8,128)(2,1)} %param.7) | copy-start | bytes 786436
  2.0 1.0 %copy-start.3 = (bf16[8,16,8,128]{3,2,1,0:T(8,128)(2,1)S(1)}, bf16[8,16,8,128]{3,2,1,0:T(8,128)(2,1)}, u32[]{:S(2)}) copy-start(bf16[8,16,8,128]{3,2,1,0:T(8,128)(2,1)} %param.6) | copy-start | bytes 786436
  2.1 1.0 %copy-start = (bf16[8,16,8,128]{3,2,1,0:T(8,128)(2,1)S(1)}, bf16[8,16,8,128]{3,2,1,0:T(8,128)(2,1)}, u32[]{:S(2)}) copy-start(bf16[8,16,8,128]{3,2,1,0:T(8,128)(2,1)} %param.11) | copy-start | bytes 786436
  2.1 1.1 %copy-start.1 = (bf16[8,16,8,128]{3,2,1,0:T(8,128)(2,1)S(1)}, bf16[8,16,8,128]{3,2,1,0:T(8,128)(2,1)}, u32[]{:S(2)}) copy-start(bf16[8,16,8,128]{3,2,1,0:T(8,128)(2,1)} %param.8) | copy-start | bytes 786436

commit v3 on v2

--- a/solution.py
+++ b/solution.py
@@ -123,16 +123,93 @@
 
 
 class Phase:
-    def __init__(self, axis, count, heads, source, gains, back, gains_back, scratch):
+    def __init__(self, axis, count, heads, source, back, scratch):
         self.axis, self.count, self.heads = axis, count, heads
-        self.source, self.gains, self.back, self.gains_back = source, gains, back, gains_back
-        (self.held, self.gains_held, self.result, self.sums, self.gains_result, self.send,
-         self.recv, self.own, self.back_send, self.back_recv, self.back_own) = scratch
+        self.source, self.back = source, back
+        (self.held, self.gains, self.gains_held, self.gains_result, self.gains_back, self.result,
+         self.sums, self.send, self.recv, self.own, self.back_send, self.back_recv,
+         self.back_own) = scratch
         self.lines = self.held.shape[1]
         self.span = self.held.shape[3]
         self.tokens = count * self.span // heads
         self.me = lax.axis_index(axis)
         self.problems = self.lines * self.tokens * heads // lanes // self.lines
+
+        self.joined = lanes // self.tokens
+
+    def placing(self, peer):
+        own = lax.broadcasted_iota(jnp.int32, (lanes, lanes), 0)
+        lane = lax.broadcasted_iota(jnp.int32, (lanes, lanes), 1)
+        token = peer * (self.span // self.heads) + own // self.heads
+        fits = (lane % self.tokens == token) & (lane // self.tokens == own % self.joined)
+        return jnp.where(fits, 1.0, 0.0).astype(bf16)
+
+    def row_masks(self):
+        table, held = self.sums.shape[0], self.gains_held.shape[1]
+        row = lax.broadcasted_iota(jnp.int32, (table, held), 0)
+        member = lax.broadcasted_iota(jnp.int32, (table, held), 1)
+        reads = jnp.where(row // self.problems == member, 1.0, 0.0).astype(bf16)
+        row = lax.broadcasted_iota(jnp.int32, (table, lanes), 0)
+        lane = lax.broadcasted_iota(jnp.int32, (table, lanes), 1)
+        return reads, lane % self.heads // self.joined == row % self.problems
+
+    def owner_maps(self, cells):
+        columns = self.lines * self.count if self.axis == "gr" else self.span // self.heads
+
+        def line_of(token):
+            return token % columns if self.axis == "gr" else token // columns
+
+        def place_of(token):
+            return token // columns if self.axis == "gr" else token % columns
+
+        token = lax.broadcasted_iota(jnp.int32, (cells, lanes), 0)
+        lane = lax.broadcasted_iota(jnp.int32, (cells, lanes), 1)
+        fits = place_of(token) == lane // self.heads
+        head = lax.broadcasted_iota(jnp.int32, (self.heads, lanes), 0)
+        lane = lax.broadcasted_iota(jnp.int32, (self.heads, lanes), 1)
+        repeat = jnp.where(lane % self.heads == head, 1.0, 0.0).astype(bf16)
+        depth = self.gains.shape[1]
+        shape = (self.count * depth, cells)
+        row = lax.broadcasted_iota(jnp.int32, shape, 0)
+        line = line_of(lax.broadcasted_iota(jnp.int32, shape, 1))
+        held = (line // self.lines == row // depth) & (line % self.lines == row % depth // 2)
+        rows = [
+            jnp.where(held & (row % 2 == kind), 1.0, 0.0).astype(bf16) for kind in range(2)
+        ]
+        return fits, repeat, rows
+
+    def offer_gains(self, kinds):
+        fits, repeat, rows = self.owner_maps(kinds[0].shape[0])
+        wide = [jnp.where(fits, dot(kind[...], repeat), 0.0) for kind in kinds]
+        packed = dot(rows[0], wide[0]) + dot(rows[1], wide[1])
+        self.gains[...] = packed.astype(bf16).reshape(self.gains.shape)
+
+    def collect_gains(self, cells):
+        fits, repeat, rows = self.owner_maps(cells)
+        packed = self.gains_back[...].reshape(-1, lanes)
+        wide = [
+            lax.dot_general(member, packed, (((0,), (0,)), ((), ())), preferred_element_type=f32)
+            for member in rows
+        ]
+        return [dot_t(jnp.where(fits, member, 0.0), repeat) for member in wide]
+
+    def unpack_gains(self):
+        reads, holds = self.row_masks()
+        table = jnp.zeros(self.sums.shape, f32)
+        for peer in range(self.count):
+            rows = jnp.where(holds, dot(reads, self.gains_held[peer]), 0.0)
+            table = table + dot(rows, self.placing(peer))
+        self.sums[...] = table
+
+    def pack_gains(self):
+        reads, holds = self.row_masks()
+        table = self.sums[...].astype(bf16)
+        for peer in range(self.count):
+            rows = jnp.where(holds, dot_t(table, self.placing(peer)), 0.0).astype(bf16)
+            packed = lax.dot_general(
+                reads, rows, (((0,), (0,)), ((), ())), preferred_element_type=f32
+            )
+            self.gains_result[peer] = packed.astype(bf16)
 
     def to(self, step):
         return lax.rem(self.me + step, self.count)
@@ -155,7 +232,7 @@
             if line < self.lines:
                 src, dst = self.result.at[to, line], self.back.at[self.me * self.lines + line]
             else:
-                src, dst = self.gains_result, self.gains_back.at[self.me]
+                src, dst = self.gains_result.at[to], self.gains_back.at[self.me]
             copies.append(
                 self.copy(src, dst, step, line, to, self.back_send, self.back_recv, self.back_own)
             )
@@ -181,13 +258,8 @@
                 stage[pl.ds(member * total + peer * span, span), :] = self.held[
                     peer, line, member
                 ].astype(f32)
-        joined = lanes // tokens
-        half = self.gains_held.shape[1] // 2
-        gains = self.gains_held[0].astype(f32)
-        for peer in range(1, self.count):
-            gains = gains + self.gains_held[peer].astype(f32)
-        if line == 0:
-            self.sums[...] = gains
+        joined = self.joined
+        first = 2 * line * self.problems
 
         def fetch(group, member):
             parts = [
@@ -199,11 +271,11 @@
         def some(index, carry):
             masks = Masks(tokens)
             groups = [index * together + extra for extra in range(together)]
-            rows = [line * self.problems + group for group in groups]
+            rows = [first + group for group in groups]
             solving = [
                 solve(
                     *(fetch(group, member) for member in range(4)),
-                    self.sums[pl.ds(row, 1), :], self.sums[pl.ds(half + row, 1), :], masks,
+                    self.sums[pl.ds(row, 1), :], self.sums[pl.ds(self.problems + row, 1), :], masks,
                 )
                 for group, row in zip(groups, rows)
             ]
@@ -213,7 +285,7 @@
                         place = pl.ds(member * total + group * joined + part, tokens, stride=heads)
                         grads[place, :] = found[member][part * tokens : (part + 1) * tokens]
                 self.sums[pl.ds(row, 1), :] = dbeta
-                self.sums[pl.ds(half + row, 1), :] = ddecay
+                self.sums[pl.ds(self.problems + row, 1), :] = ddecay
             return carry
 
         lax.fori_loop(0, self.problems // together, some, 0)
@@ -228,8 +300,8 @@
     ins, outs, scratch = refs[:4], refs[4:8], refs[8:]
     each = (len(scratch) - 2) // 2
     stage, grads = scratch[-2:]
-    row = Phase("gc", counts[0], heads, ins[0], ins[1], outs[0], outs[1], scratch[:each])
-    column = Phase("gr", counts[1], heads, ins[2], ins[3], outs[2], outs[3], scratch[each:-2])
+    row = Phase("gc", counts[0], heads, ins[0], outs[0], scratch[:each])
+    column = Phase("gr", counts[1], heads, ins[1], outs[1], scratch[each:-2])
 
     barrier = pltpu.get_barrier_semaphore()
     for phase in (row, column):
@@ -255,69 +327,59 @@
 
     arriving = {}
     for phase in (row, column):
-        arriving[phase.axis, phase.lines] = start(phase.out_copies(phase.lines))
-    for phase in (row, column):
         for line in range(phase.lines):
             arriving[phase.axis, line] = start(phase.out_copies(line))
-
-    returning = []
-    for phase in (column, row):
-        arrive(arriving[phase.axis, phase.lines])
+            if line == 0:
+                phase.offer_gains(ins[2:])
+                arriving[phase.axis, phase.lines] = start(phase.out_copies(phase.lines))
+
+    returning, gains_returning = [], []
     for line in range(max(row.lines, column.lines)):
         for phase in (column, row):
             if line >= phase.lines:
                 continue
             arrive(arriving[phase.axis, line])
+            if line == 0:
+                arrive(arriving[phase.axis, phase.lines])
+                phase.unpack_gains()
             phase.solve_line(line, stage, grads)
+            if line == phase.lines - 1:
+                phase.pack_gains()
+                gains_returning.append(start(phase.back_copies(phase.lines)))
             returning.append(start(phase.back_copies(line)))
-            if line == phase.lines - 1:
-                phase.gains_result[...] = phase.sums[...].astype(bf16)
-                returning.append(start(phase.back_copies(phase.lines)))
+    for copies in gains_returning:
+        arrive(copies)
+    found = [phase.collect_gains(ins[2].shape[0]) for phase in (row, column)]
+    for kind in range(2):
+        rounded = [member[kind].astype(bf16).astype(f32) for member in found]
+        outs[2 + kind][...] = (rounded[0] + rounded[1]).astype(bf16)
     for copies in returning:
         arrive(copies)
     for copy in started:
         copy.wait_send()
 
 
-def spread(gains, count, own, tokens, joined):
-    kinds, lines, span, heads = gains.shape
-    shaped = gains.reshape(kinds, count, lines // count, span, heads // joined, joined)
-    shaped = jnp.transpose(shaped, (1, 0, 2, 4, 5, 3))
-    mine = (jnp.arange(count) == own)[:, None]
-    placed = jnp.where(mine, shaped[..., None, :], jnp.zeros((), gains.dtype))
-    return placed.reshape(count, -1, lanes)
-
-
-def gather(gains, count, own, lines, span, heads, joined):
-    shaped = gains.reshape(count, 2, lines // count, heads // joined, joined, count, span)
-    mine = (jnp.arange(count) == own)[:, None]
-    picked = jnp.sum(jnp.where(mine, shaped.astype(f32), 0.0), axis=5)
-    return jnp.transpose(picked, (1, 0, 2, 5, 3, 4)).reshape(2, lines, span, heads)
-
-
 def on_device(counts, queries, key_vectors, values, strength, decay_rate, out_grad):
     n_row, n_col = counts
     rows, cols, heads, size = queries.shape
     row_tokens, col_tokens = n_row * cols, n_col * rows
-    row_joined, col_joined = lanes // row_tokens, lanes // col_tokens
     members = jnp.stack([queries, key_vectors, values, out_grad], axis=1)
     row_source = members.reshape(rows, 4, cols * heads, size)
     members = jnp.stack([queries, key_vectors, values, out_grad], axis=0)
     col_source = jnp.transpose(members, (2, 0, 1, 3, 4)).reshape(cols, 4, rows * heads, size)
-    gains = jnp.stack([strength, decay_rate])
-    row_own, col_own = lax.axis_index("gc"), lax.axis_index("gr")
-    row_gains = spread(gains, n_row, row_own, row_tokens, row_joined)
-    col_gains = spread(jnp.swapaxes(gains, 1, 2), n_col, col_own, col_tokens, col_joined)
-
-    def scratch(count, lines, span, gains_rows):
-        table = (gains_rows, lanes)
+
+    def scratch(count, lines, span):
+        held = (count, 2 * lines + -2 * lines % 16, lanes)
+        table = (2 * lines * count * span // lanes, lanes)
         sems = pltpu.SemaphoreType.DMA
         return [
             pltpu.VMEM((count, lines, 4, span, size), bf16),
-            pltpu.VMEM((count,) + table, bf16),
+            pltpu.VMEM(held, bf16),
+            pltpu.VMEM(held, bf16),
+            pltpu.VMEM(held, bf16),
+            pltpu.VMEM(held, bf16),
             pltpu.VMEM((count, lines, 3, span, size), bf16),
             pltpu.VMEM(table, f32),
-            pltpu.VMEM(table, bf16),
             sems((lines + 1, count - 1)),
             sems((lines + 1, count - 1)),
             sems((lines + 1,)),
@@ -329,23 +391,29 @@
     most = max(row_tokens, col_tokens) * heads
     shapes = [
         jax.ShapeDtypeStruct((rows, 3, cols * heads, size), bf16),
-        jax.ShapeDtypeStruct(row_gains.shape, bf16),
         jax.ShapeDtypeStruct((cols, 3, rows * heads, size), bf16),
-        jax.ShapeDtypeStruct(col_gains.shape, bf16),
+        jax.ShapeDtypeStruct((rows * cols, heads), bf16),
+        jax.ShapeDtypeStruct((rows * cols, heads), bf16),
     ]
-    row_back, row_gains_back, col_back, col_gains_back = pl.pallas_call(
+    places = [pl.BlockSpec(memory_space=pl.ANY)] * 2 + [pl.BlockSpec(memory_space=pltpu.VMEM)] * 2
+    row_back, col_back, strength_grad, decay_grad = pl.pallas_call(
         functools.partial(kernel, counts, heads),
         out_shape=shapes,
-        in_specs=[pl.BlockSpec(memory_space=pl.ANY)] * 4,
-        out_specs=[pl.BlockSpec(memory_space=pl.ANY)] * 4,
-        scratch_shapes=scratch(n_row, rows // n_row, cols * heads, row_gains.shape[1])
-        + scratch(n_col, cols // n_col, rows * heads, col_gains.shape[1])
+        in_specs=places,
+        out_specs=places,
+        scratch_shapes=scratch(n_row, rows // n_row, cols * heads)
+        + scratch(n_col, cols // n_col, rows * heads)
         + [pltpu.VMEM((4 * most, size), f32), pltpu.VMEM((3 * most, size), f32)],
         compiler_params=pltpu.CompilerParams(
             collective_id=0, has_side_effects=True, vmem_limit_bytes=40 * 2**20
         ),
         name="exchange_and_solve",
-    )(row_source, row_gains, col_source, col_gains)
+    )(
+        row_source,
+        col_source,
+        strength.reshape(rows * cols, heads),
+        decay_rate.reshape(rows * cols, heads),
+    )
 
     row_back = row_back.reshape(rows, 3, cols, heads, size)
     col_back = col_back.reshape(cols, 3, rows, heads, size)
@@ -355,9 +423,7 @@
         second = jnp.swapaxes(col_back[:, member], 0, 1).astype(f32)
         return (first + second).astype(bf16)
 
-    row_small = gather(row_gains_back, n_row, row_own, rows, cols, heads, row_joined)
-    col_small = gather(col_gains_back, n_col, col_own, cols, rows, heads, col_joined)
-    small = (row_small + jnp.swapaxes(col_small, 1, 2)).astype(bf16)
+    small = [member.reshape(rows, cols, heads) for member in (strength_grad, decay_grad)]
     return (merged(0), merged(1), merged(2), small[0], small[1])
 
 

time: 56.3 us -> 53.4 us (0.948)
  Pallas kernels: 48.9 us -> 47.3 us
  local copies, waits for them, and re-layouts: 3.89 us -> 2.39 us
    pallas_call x1, Pallas kernels: 48.9 us -> 47.3 us  [on_device(): pl.pallas_call(functools.partial(kernel, counts, heads), out_shape=shapes...]
    another operation x1, other arithmetic: 0.13 us -> 1.4 us  [on_device(): members = jnp.stack([queries, key_vectors, values, out_grad], axis=1)]
    unnamed x14, local copies, waits for them, and re-layouts: 1.12 us -> 2.33 us
    broadcast_in_dim x8 -> x0, local copies, waits for them, and re-layouts: 1.13 us -> none  [spread(): placed = jnp.where(mine, shaped[..., None, :], jnp.zeros((), gains.dtype))]
    convert_element_type x2 -> x0, local copies, waits for them, and re-layouts: 0.77 us -> none  [gather(): picked = jnp.sum(jnp.where(mine, shaped.astype(f32), 0.0), axis=5)]
    reduce_sum x2 -> x0, other arithmetic: 0.72 us -> none  [gather(): picked = jnp.sum(jnp.where(mine, shaped.astype(f32), 0.0), axis=5)]
    squeeze x1 -> x0, local copies, waits for them, and re-layouts: 0.61 us -> none  [on_device(): return (merged(0), merged(1), merged(2), small[0], small[1])]
where the time goes in v3:
time: 53.4 us; the launch traced here: 53.1 us
  Pallas kernels  47.3 us (89%)
  other arithmetic  2.7 us (5%)
  local copies, waits for them, and re-layouts  2.39 us (4%)
  between operations  0.73 us (1%)
    pallas_call x1, Pallas kernels, on_device(): pl.pallas_call(functools.partial(kernel, counts, heads), out_shape=shapes...  47.3 us
    unnamed x14, local copies, waits for them, and re-layouts  2.33 us
    another operation x1, other arithmetic, on_device(): members = jnp.stack([queries, key_vectors, values, out_grad], axis=1)  1.4 us

profile of v3, /device:TPU:0, one launch (start us, length us, event | category | flops | bytes accessed | tf_op | source)
XLA Modules:
  0.0 53.1 jit_solution(7958044192693871399)
XLA Ops:
  0.6 0.0 copy-start.4
  0.6 0.8 %copy.12 = bf16[8,16,8]{2,1,0:T(8,128)(2,1)S(1)} copy(bf16[8,16,8]{1,2,0:T(8,128)(2,1)} %param.9) | data formatting | bytes 4096 | tf_op args[3]
  1.4 0.0 copy-done.4
  1.5 0.1 copy.13
  1.6 0.0 copy-start
  1.6 0.0 copy-start.1
  1.6 0.0 copy-start.2
  1.6 0.0 copy-start.3
  1.6 1.4 %pad_maximum_fusion.refs_0_ = bf16[8,4,128,128]{3,2,1,0:T(8,128)(2,1)S(1)} fusion(bf16[8,1,128,128]{3,2,1,0:T(8,128)(2,1)} %bitcast.79, bf16[8,1,128,128]{3,2,1,0:T(8,128)(2,1)} %bitcast.81, bf16[8,1,128,128]{3,2,1,0:T(8,128)(2,1)} %bitcast.83, bf16[8,1,128,128]{3,2,1,0:T(8,128)(2,1)} %bitcast.85), kind=kLoop, calls=%fused_computation | loop fusion | flops 1572864 | bytes 2097152 | tf_op jit(solution)/shard_map/stack | solution.py:366
  3.0 0.0 copy-done
  3.0 0.0 copy-done.1
  3.0 0.0 copy-done.2
  3.0 0.0 copy-done.3
  3.1 0.3 copy_bitcast_fusion.refs_1_
  3.4 47.3 %exchange_and_solve.1 = (bf16[8,3,128,128]{3,2,1,0:T(8,128)(2,1)S(1)}, bf16[16,3,64,128]{3,2,1,0:T(8,128)(2,1)S(1)}, bf16[128,8]{1,0:T(8,128)(2,1)S(1)}, bf16[128,8]{1,0:T(8,128)(2,1)S(1)}) custom-call(bf16[8,4,128,128]{3,2,1,0:T(8,128)(2,1)S(1)} %pad_maximum_fusion.refs_0_, bf16[16,4,64,128]{3,2,1,0:T(8,128)(2,1)S(1)} %copy_bitcast_fusion.refs_1_, ...), custom_call_target="tpu_custom_call" | custom-call | tf_op jit(solution)/shard_map/exchange_and_solve/pallas_call | solution.py:399
  50.6 0.1 fusion.6
  50.7 1.0 %fusion.1 = (bf16[8,16,8,128]{3,2,1,0:T(8,128)(2,1)}, bf16[8,16,8,128]{3,2,1,0:T(8,128)(2,1)}, bf16[8,16,8,128]{3,2,1,0:T(8,128)(2,1)}) fusion(bf16[8,3,16,8,128]{4,3,2,1,0:T(8,128)(2,1)S(1)} %bitcast.74, bf16[16,1,8,8,128]{4,3,2,1,0:T(8,128)(2,1)S(1)} %get-tuple-element.21, bf16[16,1,8,8,128]{4,3,2,1,0:T(8,128)(2,1)S(1)} %get-tuple-element.22, ...), kind=kLoop, calls=%fused_computation.5 | loop fusion | flops 1572864 | bytes 2359296 | tf_op jit(solution)/shard_map/convert_element_type | solution.py:424
  51.7 0.7 %copy.20 = bf16[8,16,8]{1,2,0:T(8,128)(2,1)} copy(bf16[8,16,8]{2,1,0:T(8,128)(2,1)S(1)} %bitcast.78) | data formatting | bytes 4096
  52.4 0.7 %copy.21 = bf16[8,16,8]{1,2,0:T(8,128)(2,1)} copy(bf16[8,16,8]{2,1,0:T(8,128)(2,1)S(1)} %bitcast.77) | data formatting | bytes 4096
Async XLA Ops:
  0.6 0.8 %copy-start.4 = (bf16[8,16,8]{1,2,0:T(8,128)(2,1)S(1)}, bf16[8,16,8]{1,2,0:T(8,128)(2,1)}, u32[]{:S(2)}) copy-start(bf16[8,16,8]{1,2,0:T(8,128)(2,1)} %param.10) | copy-start | bytes 6148
  1.6 1.5 %copy-start = (bf16[8,16,8,128]{3,2,1,0:T(8,128)(2,1)S(1)}, bf16[8,16,8,128]{3,2,1,0:T(8,128)(2,1)}, u32[]{:S(2)}) copy-start(bf16[8,16,8,128]{3,2,1,0:T(8,128)(2,1)} %param.11) | copy-start | bytes 786436
  1.6 1.5 %copy-start.1 = (bf16[8,16,8,128]{3,2,1,0:T(8,128)(2,1)S(1)}, bf16[8,16,8,128]{3,2,1,0:T(8,128)(2,1)}, u32[]{:S(2)}) copy-start(bf16[8,16,8,128]{3,2,1,0:T(8,128)(2,1)} %param.8) | copy-start | bytes 786436
  1.6 1.4 %copy-start.2 = (bf16[8,16,8,128]{3,2,1,0:T(8,128)(2,1)S(1)}, bf16[8,16,8,128]{3,2,1,0:T(8,128)(2,1)}, u32[]{:S(2)}) copy-start(bf16[8,16,8,128]{3,2,1,0:T(8,128)(2,1)} %param.7) | copy-start | bytes 786436
  1.6 1.5 %copy-start.3 = (bf16[8,16,8,128]{3,2,1,0:T(8,128)(2,1)S(1)}, bf16[8,16,8,128]{3,2,1,0:T(8,128)(2,1)}, u32[]{:S(2)}) copy-start(bf16[8,16,8,128]{3,2,1,0:T(8,128)(2,1)} %param.6) | copy-start | bytes 786436

commit v4 on v3

--- a/solution.py
+++ b/solution.py
@@ -180,7 +180,7 @@
 
     def offer_gains(self, kinds):
         fits, repeat, rows = self.owner_maps(kinds[0].shape[0])
-        wide = [jnp.where(fits, dot(kind[...], repeat), 0.0) for kind in kinds]
+        wide = [jnp.where(fits, dot(kind, repeat), 0.0) for kind in kinds]
         packed = dot(rows[0], wide[0]) + dot(rows[1], wide[1])
         self.gains[...] = packed.astype(bf16).reshape(self.gains.shape)
 
@@ -330,7 +330,7 @@
         for line in range(phase.lines):
             arriving[phase.axis, line] = start(phase.out_copies(line))
             if line == 0:
-                phase.offer_gains(ins[2:])
+                phase.offer_gains([kind[...].astype(f32).reshape(-1, heads) for kind in ins[2:]])
                 arriving[phase.axis, phase.lines] = start(phase.out_copies(phase.lines))
 
     returning, gains_returning = [], []
@@ -349,10 +349,12 @@
             returning.append(start(phase.back_copies(line)))
     for copies in gains_returning:
         arrive(copies)
-    found = [phase.collect_gains(ins[2].shape[0]) for phase in (row, column)]
+    cells = ins[2].shape[0] * ins[2].shape[1]
+    found = [phase.collect_gains(cells) for phase in (row, column)]
     for kind in range(2):
         rounded = [member[kind].astype(bf16).astype(f32) for member in found]
-        outs[2 + kind][...] = (rounded[0] + rounded[1]).astype(bf16)
+        total = (rounded[0] + rounded[1]).reshape(outs[2 + kind].shape)
+        outs[2 + kind][...] = total.astype(bf16)
     for copies in returning:
         arrive(copies)
     for copy in started:
@@ -392,8 +394,8 @@
     shapes = [
         jax.ShapeDtypeStruct((rows, 3, cols * heads, size), bf16),
         jax.ShapeDtypeStruct((cols, 3, rows * heads, size), bf16),
-        jax.ShapeDtypeStruct((rows * cols, heads), bf16),
-        jax.ShapeDtypeStruct((rows * cols, heads), bf16),
+        jax.ShapeDtypeStruct((rows, cols, heads), bf16),
+        jax.ShapeDtypeStruct((rows, cols, heads), bf16),
     ]
     places = [pl.BlockSpec(memory_space=pl.ANY)] * 2 + [pl.BlockSpec(memory_space=pltpu.VMEM)] * 2
     row_back, col_back, strength_grad, decay_grad = pl.pallas_call(
@@ -411,8 +413,8 @@
     )(
         row_source,
         col_source,
-        strength.reshape(rows * cols, heads),
-        decay_rate.reshape(rows * cols, heads),
+        strength,
+        decay_rate,
     )
 
     row_back = row_back.reshape(rows, 3, cols, heads, size)
@@ -423,8 +425,7 @@
         second = jnp.swapaxes(col_back[:, member], 0, 1).astype(f32)
         return (first + second).astype(bf16)
 
-    small = [member.reshape(rows, cols, heads) for member in (strength_grad, decay_grad)]
-    return (merged(0), merged(1), merged(2), small[0], small[1])
+    return (merged(0), merged(1), merged(2), strength_grad, decay_grad)
 
 
 def solution(mesh):

time: 53.4 us -> 53.4 us (level)
  no operation moved by 1% of the time
where the time goes in v4:
time: 53.4 us; the launch traced here: 53.1 us
  Pallas kernels  47.3 us (89%)
  other arithmetic  2.7 us (5%)
  local copies, waits for them, and re-layouts  2.39 us (4%)
  between operations  0.73 us (1%)
    pallas_call x1, Pallas kernels, on_device(): pl.pallas_call(functools.partial(kernel, counts, heads), out_shape=shapes...  47.3 us
    unnamed x14, local copies, waits for them, and re-layouts  2.33 us
    another operation x1, other arithmetic, on_device(): members = jnp.stack([queries, key_vectors, values, out_grad], axis=1)  1.4 us

profile of v4, /device:TPU:0, one launch (start us, length us, event | category | flops | bytes accessed | tf_op | source)
XLA Modules:
  0.0 53.1 jit_solution(7958044192693871399)
XLA Ops:
  0.6 0.0 copy-start.4
  0.6 0.8 %copy.12.refs_2_ = bf16[8,16,8]{2,1,0:T(8,128)(2,1)S(1)} copy(bf16[8,16,8]{1,2,0:T(8,128)(2,1)} %param.9) | data formatting | bytes 4096 | tf_op args[3]
  1.4 0.0 copy-done.4
  1.5 0.1 copy.13.refs_3_
  1.6 0.0 copy-start
  1.6 0.0 copy-start.1
  1.6 0.0 copy-start.2
  1.6 0.0 copy-start.3
  1.6 1.4 %pad_maximum_fusion.refs_0_ = bf16[8,4,128,128]{3,2,1,0:T(8,128)(2,1)S(1)} fusion(bf16[8,1,128,128]{3,2,1,0:T(8,128)(2,1)} %bitcast.71, bf16[8,1,128,128]{3,2,1,0:T(8,128)(2,1)} %bitcast.73, bf16[8,1,128,128]{3,2,1,0:T(8,128)(2,1)} %bitcast.75, bf16[8,1,128,128]{3,2,1,0:T(8,128)(2,1)} %bitcast.77), kind=kLoop, calls=%fused_computation | loop fusion | flops 1572864 | bytes 2097152 | tf_op jit(solution)/shard_map/stack | solution.py:368
  3.0 0.0 copy-done
  3.0 0.0 copy-done.1
  3.0 0.0 copy-done.2
  3.0 0.0 copy-done.3
  3.1 0.3 copy_bitcast_fusion.refs_1_
  3.4 47.3 %exchange_and_solve.1 = (bf16[8,3,128,128]{3,2,1,0:T(8,128)(2,1)S(1)}, bf16[16,3,64,128]{3,2,1,0:T(8,128)(2,1)S(1)}, bf16[8,16,8]{2,1,0:T(8,128)(2,1)S(1)}, bf16[8,16,8]{2,1,0:T(8,128)(2,1)S(1)}) custom-call(bf16[8,4,128,128]{3,2,1,0:T(8,128)(2,1)S(1)} %pad_maximum_fusion.refs_0_, bf16[16,4,64,128]{3,2,1,0:T(8,128)(2,1)S(1)} %copy_bitcast_fusion.refs_1_, ...), custom_call_target="tpu_custom_call" | custom-call | tf_op jit(solution)/shard_map/exchange_and_solve/pallas_call | solution.py:401
  50.6 0.1 fusion.6
  50.7 1.0 %fusion.1 = (bf16[8,16,8,128]{3,2,1,0:T(8,128)(2,1)}, bf16[8,16,8,128]{3,2,1,0:T(8,128)(2,1)}, bf16[8,16,8,128]{3,2,1,0:T(8,128)(2,1)}) fusion(bf16[8,3,16,8,128]{4,3,2,1,0:T(8,128)(2,1)S(1)} %bitcast.70, bf16[16,1,8,8,128]{4,3,2,1,0:T(8,128)(2,1)S(1)} %get-tuple-element.21, bf16[16,1,8,8,128]{4,3,2,1,0:T(8,128)(2,1)S(1)} %get-tuple-element.22, ...), kind=kLoop, calls=%fused_computation.5 | loop fusion | flops 1572864 | bytes 2359296 | tf_op jit(solution)/shard_map/convert_element_type | solution.py:426
  51.7 0.7 %copy.20 = bf16[8,16,8]{1,2,0:T(8,128)(2,1)} copy(bf16[8,16,8]{2,1,0:T(8,128)(2,1)S(1)} %get-tuple-element.16) | data formatting | bytes 4096
  52.4 0.7 %copy.21 = bf16[8,16,8]{1,2,0:T(8,128)(2,1)} copy(bf16[8,16,8]{2,1,0:T(8,128)(2,1)S(1)} %get-tuple-element.17) | data formatting | bytes 4096
Async XLA Ops:
  0.6 0.8 %copy-start.4 = (bf16[8,16,8]{1,2,0:T(8,128)(2,1)S(1)}, bf16[8,16,8]{1,2,0:T(8,128)(2,1)}, u32[]{:S(2)}) copy-start(bf16[8,16,8]{1,2,0:T(8,128)(2,1)} %param.10) | copy-start | bytes 6148
  1.6 1.5 %copy-start = (bf16[8,16,8,128]{3,2,1,0:T(8,128)(2,1)S(1)}, bf16[8,16,8,128]{3,2,1,0:T(8,128)(2,1)}, u32[]{:S(2)}) copy-start(bf16[8,16,8,128]{3,2,1,0:T(8,128)(2,1)} %param.11) | copy-start | bytes 786436
  1.6 1.5 %copy-start.1 = (bf16[8,16,8,128]{3,2,1,0:T(8,128)(2,1)S(1)}, bf16[8,16,8,128]{3,2,1,0:T(8,128)(2,1)}, u32[]{:S(2)}) copy-start(bf16[8,16,8,128]{3,2,1,0:T(8,128)(2,1)} %param.8) | copy-start | bytes 786436
  1.6 1.4 %copy-start.2 = (bf16[8,16,8,128]{3,2,1,0:T(8,128)(2,1)S(1)}, bf16[8,16,8,128]{3,2,1,0:T(8,128)(2,1)}, u32[]{:S(2)}) copy-start(bf16[8,16,8,128]{3,2,1,0:T(8,128)(2,1)} %param.7) | copy-start | bytes 786436
  1.6 1.5 %copy-start.3 = (bf16[8,16,8,128]{3,2,1,0:T(8,128)(2,1)S(1)}, bf16[8,16,8,128]{3,2,1,0:T(8,128)(2,1)}, u32[]{:S(2)}) copy-start(bf16[8,16,8,128]{3,2,1,0:T(8,128)(2,1)} %param.6) | copy-start | bytes 786436
